TPU v7x, 256 devices: a whole 4x4x8 slice. The times are simulated.
256 devices in a mesh: sec: 8 (over y, x_lo), ty: 4 (over x_hi, core), tx: 8 (over z).
Axes of the slice: x: 4 (x_hi: 2, x_lo: 2; x = x_hi * 2 + x_lo), y: 4, z: 8, core: 2. Of those that a mesh axis runs over, the one named last changes fastest.
Arguments:
- images: float32 [8, 1024, 4096], P('sec', 'ty', 'tx'), may hold values from -12 to 12
Outputs:
- relaxed: float32 [8, 2, 16, 64], P('sec', None, 'ty', 'tx')
- cumulative: float32 [8, 2, 16, 64], P('sec', None, 'ty', 'tx')
All inputs are finite; a program needn't handle non-finite values.
Results may differ from a plain program's by a relative error of at most 0.0003.
Values sent between devices are 32-bit elements; how exact they have to be, the bound alone decides.
A program may use at most 64 MiB of HBM per device.

v0:
```python
import math

import jax
import jax.numpy as jnp
from jax import lax
from jax.sharding import PartitionSpec as P

PATCH = 128
STRIDE = 64


stiffness = 1.0
rate = 0.25


def shifted(value, axis, by):
    length = lax.axis_size(axis)
    pairs = [(i, i + by) for i in range(length) if 0 <= i + by < length]
    return lax.ppermute(value, axis, pairs)


def padded_2(value, sides, width):
    for axis, dim in sides:
        size, length = (lax.axis_size(axis), value.shape[dim])
        up = [(i, (i + 1) % size) for i in range(size - 1)]
        down = [(j, i) for i, j in up]
        last = lax.slice_in_dim(value, length - width, length, axis=dim)
        first = lax.slice_in_dim(value, 0, width, axis=dim)
        before = lax.ppermute(last, axis, up)
        after = lax.ppermute(first, axis, down)
        value = jnp.concatenate([before, value, after], axis=dim)
    return value


def from_everyone(value, axis):
    length = lax.axis_size(axis)
    return lax.all_to_all(
        jnp.broadcast_to(value[None], (length, *value.shape)), axis, 0, 0, tiled=True
    )


def joined_by_halves(pieces, combine):
    while len(jax.tree.leaves(pieces)[0]) > 1:
        pieces = jax.vmap(combine)(*(pieces[side::2] for side in (0, 1)))
    return pieces[0]


def prefix(value, axis, combine, identity):
    length, position = (lax.axis_size(axis), lax.axis_index(axis))
    passed = jnp.arange(length) < position

    def kept(part, zero, own):
        part = jnp.where(
            passed.reshape(-1, *(1 for _ in own.shape)), part, jnp.asarray(zero, own.dtype)
        )
        return part

    pieces = from_everyone(value, axis)
    return joined_by_halves(kept(pieces, identity, value), combine)


def left_apply(table, values):
    return jnp.einsum("jk,snkl->snjl", table, values, precision=lax.Precision.HIGHEST)


def right_apply(values, table):
    return jnp.einsum("snjk,kl->snjl", values, table, precision=lax.Precision.HIGHEST)


def soft_flow(corr):
    count = corr.shape[0]
    scores = corr / PATCH
    weights = jax.nn.softmax(scores.reshape(count, PATCH * PATCH), axis=-1).reshape(
        count, PATCH, PATCH
    )
    offsets = jnp.arange(PATCH)
    offsets = jnp.where(offsets < PATCH // 2, offsets, offsets - PATCH).astype(jnp.float32)
    flow_y = jnp.sum(weights * offsets[:, None], axis=(1, 2))
    flow_x = jnp.sum(weights * offsets[None, :], axis=(1, 2))
    return jnp.stack([flow_y, flow_x])


def band_flow(bands, cosines, sines):
    nodes = bands.shape[2] // STRIDE - 1
    columns = bands.reshape(2, PATCH, nodes + 1, STRIDE)
    pieces = jnp.concatenate([columns[:, :, :-1], columns[:, :, 1:]], axis=3)
    pieces = jnp.transpose(pieces, (0, 2, 1, 3))
    pieces = pieces - jnp.mean(pieces, axis=(2, 3), keepdims=True)
    left_real = left_apply(cosines, pieces)
    left_imag = -left_apply(sines, pieces)
    freq_real = right_apply(left_real, cosines) + right_apply(left_imag, sines)
    freq_imag = right_apply(left_imag, cosines) - right_apply(left_real, sines)
    prod_real = freq_real[0] * freq_real[1] + freq_imag[0] * freq_imag[1]
    prod_imag = freq_real[0] * freq_imag[1] - freq_imag[0] * freq_real[1]
    prods = jnp.stack([prod_real, prod_imag])
    mixed_real = left_apply(cosines, prods[:1]) - left_apply(sines, prods[1:])
    mixed_imag = left_apply(sines, prods[:1]) + left_apply(cosines, prods[1:])
    corr = (right_apply(mixed_real, cosines) - right_apply(mixed_imag, sines))[0] / (PATCH * PATCH)
    return soft_flow(corr)


def lap_of(padded, center):
    return (
        padded[:, :-2, 1:-1]
        + padded[:, 2:, 1:-1]
        + padded[:, 1:-1, :-2]
        + padded[:, 1:-1, 2:]
        - 4.0 * center
    )


def on_device(images):
    own_tile = images[0]
    half = STRIDE // 2
    next_tile = shifted(own_tile, "sec", -1)
    haloed = padded_2(jnp.stack([own_tile, next_tile]), (("ty", 1), ("tx", 2)), half)
    node_rows = own_tile.shape[0] // STRIDE
    node_cols = own_tile.shape[1] // STRIDE
    grid = jnp.arange(PATCH, dtype=jnp.int32)
    angles = (grid[:, None] * grid[None, :] % PATCH).astype(jnp.float32) * (2.0 * math.pi / PATCH)
    cosines = jnp.cos(angles)
    sines = jnp.sin(angles)
    strips = haloed.reshape(2, node_rows + 1, STRIDE, haloed.shape[2])
    bands = jnp.concatenate([strips[:, :-1], strips[:, 1:]], axis=2)
    bands = jnp.transpose(bands, (1, 0, 2, 3))
    rows = lax.map(lambda band: band_flow(band, cosines, sines), bands)
    flow = jnp.transpose(rows, (1, 0, 2))
    keep = (lax.axis_index("sec") < lax.axis_size("sec") - 1).astype(jnp.float32)
    flow = flow * keep
    padded = padded_2(flow, (("ty", 1), ("tx", 2)), 2)
    inner = padded[:, 1:-1, 1:-1]
    first = inner + rate * (stiffness * lap_of(padded, inner) + inner - inner)
    row_ids = lax.axis_index("ty") * node_rows + jnp.arange(-1, node_rows + 1, dtype=jnp.int32)
    col_ids = lax.axis_index("tx") * node_cols + jnp.arange(-1, node_cols + 1, dtype=jnp.int32)
    row_ok = (row_ids >= 0) & (row_ids < node_rows * lax.axis_size("ty"))
    col_ok = (col_ids >= 0) & (col_ids < node_cols * lax.axis_size("tx"))
    inside = (row_ok[:, None] & col_ok[None, :]).astype(jnp.float32)
    first = first * inside[None]
    center = first[:, 1:-1, 1:-1]
    mesh = center + rate * (stiffness * lap_of(first, center) + flow - center)
    earlier = prefix(mesh, "sec", lambda early, late: early + late, jnp.zeros_like(mesh))
    return (mesh[None], earlier[None])


def solution(mesh):
    in_specs = (P("sec", "ty", "tx"),)
    out_specs = (P("sec", None, "ty", "tx"), P("sec", None, "ty", "tx"))
    return jax.shard_map(
        on_device, mesh=mesh, in_specs=in_specs, out_specs=out_specs, check_vma=False
    )
```

profile of v0, /device:TPU:92, one launch (start us, length us, event | category | flops | bytes accessed | tf_op | source)
XLA Modules:
  0.0 149.8 jit_solution(6935601763260787447)
XLA Ops:
  0.6 3.4 %collective-permute-start = (f32[256,512]{1,0:T(8,128)}, f32[256,512]{1,0:T(8,128)S(1)}, u32[]{:S(2)}, u32[]{:S(2)}) collective-permute-start(f32[256,512]{1,0:T(8,128)} %bitcast.162), channel_id=1, source_target_pairs={{32,0},{64,32},{96,64},{128,96},{160,128},{192,160},{224,192},{33,... | collective-permute-start | bytes 1572872 | tf_op jit(solution)/shard_map/ppermute | solution.py:19
  4.1 12.5 %collective-permute-done = f32[256,512]{1,0:T(8,128)S(1)} collective-permute-done((f32[256,512]{1,0:T(8,128)}, f32[256,512]{1,0:T(8,128)S(1)}, u32[]{:S(2)}, u32[]{:S(2)}) %collective-permute-start) | collective-permute-done | bytes 524320 | tf_op jit(solution)/shard_map/ppermute | solution.py:19
  19.4 5.1 %collective-permute-start.2 = (f32[2,32,512]{2,1,0:T(8,128)S(1)}, f32[2,32,512]{2,1,0:T(8,128)S(1)}, u32[]{:S(2)}, u32[]{:S(2)}) collective-permute-start(f32[2,32,512]{2,1,0:T(8,128)S(1)} %get-tuple-element.174), channel_id=1, source_target_pairs={{8,0},{16,8},{24,16},{9,1},{17,9},{25,17},{10,2},{18,10},{26,18},{... | collective-permute-start | bytes 393224 | tf_op jit(solution)/shard_map/ppermute | solution.py:30
  27.2 3.8 %collective-permute-start.3 = (f32[2,320,32]{2,1,0:T(8,128)S(1)}, f32[2,320,32]{2,1,0:T(8,128)S(1)}, u32[]{:S(2)}, u32[]{:S(2)}) collective-permute-start(f32[2,320,32]{2,1,0:T(8,128)S(1)} %get-tuple-element.171), channel_id=1, source_target_pairs={{0,1},{1,2},{2,3},{3,4},{4,5},{5,6},{6,7},{8,9},{9,10},{10,11},{11... | collective-permute-start | bytes 245768 | tf_op jit(solution)/shard_map/ppermute | solution.py:29
  31.0 2.0 %collective-permute-start.4 = (f32[2,320,32]{2,1,0:T(8,128)S(1)}, f32[2,320,32]{2,1,0:T(8,128)S(1)}, u32[]{:S(2)}, u32[]{:S(2)}) collective-permute-start(f32[2,320,32]{2,1,0:T(8,128)S(1)} %get-tuple-element.172), channel_id=1, source_target_pairs={{1,0},{2,1},{3,2},{4,3},{5,4},{6,5},{7,6},{9,8},{10,9},{11,10},{12... | collective-permute-start | bytes 245768 | tf_op jit(solution)/shard_map/ppermute | solution.py:30
  33.1 3.1 %collective-permute-done.3 = f32[2,320,32]{2,1,0:T(8,128)S(1)} collective-permute-done((f32[2,320,32]{2,1,0:T(8,128)S(1)}, f32[2,320,32]{2,1,0:T(8,128)S(1)}, u32[]{:S(2)}, u32[]{:S(2)}) %collective-permute-start.3) | collective-permute-done | bytes 81952 | tf_op jit(solution)/shard_map/ppermute | solution.py:29
  36.2 4.9 %collective-permute-done.4 = f32[2,320,32]{2,1,0:T(8,128)S(1)} collective-permute-done((f32[2,320,32]{2,1,0:T(8,128)S(1)}, f32[2,320,32]{2,1,0:T(8,128)S(1)}, u32[]{:S(2)}, u32[]{:S(2)}) %collective-permute-start.4) | collective-permute-done | bytes 81952 | tf_op jit(solution)/shard_map/ppermute | solution.py:30
  43.6 2.1 %copy.25 = f32[4,2,128,576]{2,3,1,0:T(8,128)S(1)} copy(f32[4,2,128,576]{3,2,0,1:T(8,128)} %maximum_bitcast_fusion.4) | data formatting | bytes 4718592
  45.8 72.8 %while.15 = (s32[]{:T(128)}, f32[4,2,8]{2,1,0:T(2,128)S(1)}, f32[4,2,128,576]{2,3,1,0:T(8,128)S(1)}, s32[]{:T(128)}) while((s32[]{:T(128)}, f32[4,2,8]{2,1,0:T(2,128)S(1)}, f32[4,2,128,576]{2,3,1,0:T(8,128)S(1)}, s32[]{:T(128)}) %tuple.59), condition=%wide.region_6.7_spmd.clone.clone, body=%wide.region_0.6_spmd.clone.clone.sunk | while | flops 3631481344 | bytes 31067740 | solution.py:126
  47.4 1.9 %fusion.194 = f32[2,8,128,128]{3,2,1,0:T(8,128)S(1)} fusion(f32[2,8,128,128]{2,3,1,0:T(8,128)S(1)} %convolution_bitcast_fusion.2), kind=kOutput, calls=%fused_computation.50.clone.1 | convolution fusion | flops 402882560 | bytes 2097152 | tf_op jit(solution)/shard_map/while/body/eval_jaxpr/snjk,kl->snjl/dot_general | solution.py:67
  50.5 1.9 %convolution_add_fusion.3 = f32[2,8,128,128]{3,2,1,0:T(8,128)S(1)} fusion(f32[2,8,128,128]{3,2,1,0:T(8,128)S(1)} %fusion.194, f32[2,8,128,128]{2,3,1,0:T(8,128)S(1)} %fusion.192), kind=kOutput, calls=%fused_computation.3.clone.1 | convolution fusion | flops 403144704 | bytes 3145728 | tf_op jit(solution)/shard_map/while/body/eval_jaxpr/snjk,kl->snjl/dot_general | solution.py:67
  52.5 1.9 %fusion.193 = f32[2,8,128,128]{3,2,1,0:T(8,128)S(1)} fusion(f32[2,8,128,128]{2,3,1,0:T(8,128)S(1)} %fusion.192), kind=kOutput, calls=%fused_computation.48.clone.1 | convolution fusion | flops 402882560 | bytes 2097152 | tf_op jit(solution)/shard_map/while/body/eval_jaxpr/snjk,kl->snjl/dot_general | solution.py:67
  65.6 1.9 %fusion.194 = f32[2,8,128,128]{3,2,1,0:T(8,128)S(1)} fusion(f32[2,8,128,128]{2,3,1,0:T(8,128)S(1)} %convolution_bitcast_fusion.2), kind=kOutput, calls=%fused_computation.50.clone.1 | convolution fusion | flops 402882560 | bytes 2097152 | tf_op jit(solution)/shard_map/while/body/eval_jaxpr/snjk,kl->snjl/dot_general | solution.py:67
  70.7 1.9 %fusion.193 = f32[2,8,128,128]{3,2,1,0:T(8,128)S(1)} fusion(f32[2,8,128,128]{2,3,1,0:T(8,128)S(1)} %fusion.192), kind=kOutput, calls=%fused_computation.48.clone.1 | convolution fusion | flops 402882560 | bytes 2097152 | tf_op jit(solution)/shard_map/while/body/eval_jaxpr/snjk,kl->snjl/dot_general | solution.py:67
  83.8 1.9 %fusion.194 = f32[2,8,128,128]{3,2,1,0:T(8,128)S(1)} fusion(f32[2,8,128,128]{2,3,1,0:T(8,128)S(1)} %convolution_bitcast_fusion.2), kind=kOutput, calls=%fused_computation.50.clone.1 | convolution fusion | flops 402882560 | bytes 2097152 | tf_op jit(solution)/shard_map/while/body/eval_jaxpr/snjk,kl->snjl/dot_general | solution.py:67
  88.9 1.9 %fusion.193 = f32[2,8,128,128]{3,2,1,0:T(8,128)S(1)} fusion(f32[2,8,128,128]{2,3,1,0:T(8,128)S(1)} %fusion.192), kind=kOutput, calls=%fused_computation.48.clone.1 | convolution fusion | flops 402882560 | bytes 2097152 | tf_op jit(solution)/shard_map/while/body/eval_jaxpr/snjk,kl->snjl/dot_general | solution.py:67
  102.0 1.9 %fusion.194 = f32[2,8,128,128]{3,2,1,0:T(8,128)S(1)} fusion(f32[2,8,128,128]{2,3,1,0:T(8,128)S(1)} %convolution_bitcast_fusion.2), kind=kOutput, calls=%fused_computation.50.clone.1 | convolution fusion | flops 402882560 | bytes 2097152 | tf_op jit(solution)/shard_map/while/body/eval_jaxpr/snjk,kl->snjl/dot_general | solution.py:67
  105.1 1.9 %convolution_add_fusion.3 = f32[2,8,128,128]{3,2,1,0:T(8,128)S(1)} fusion(f32[2,8,128,128]{3,2,1,0:T(8,128)S(1)} %fusion.194, f32[2,8,128,128]{2,3,1,0:T(8,128)S(1)} %fusion.192), kind=kOutput, calls=%fused_computation.3.clone.1 | convolution fusion | flops 403144704 | bytes 3145728 | tf_op jit(solution)/shard_map/while/body/eval_jaxpr/snjk,kl->snjl/dot_general | solution.py:67
  107.1 1.9 %fusion.193 = f32[2,8,128,128]{3,2,1,0:T(8,128)S(1)} fusion(f32[2,8,128,128]{2,3,1,0:T(8,128)S(1)} %fusion.192), kind=kOutput, calls=%fused_computation.48.clone.1 | convolution fusion | flops 402882560 | bytes 2097152 | tf_op jit(solution)/shard_map/while/body/eval_jaxpr/snjk,kl->snjl/dot_general | solution.py:67
  120.5 5.1 %collective-permute-start.6 = (f32[2,2,8]{2,0,1:T(2,128)S(1)}, f32[2,2,8]{2,0,1:T(2,128)S(1)}, u32[]{:S(2)}, u32[]{:S(2)}) collective-permute-start(f32[2,2,8]{2,0,1:T(2,128)S(1)} %get-tuple-element.180), channel_id=1, source_target_pairs={{8,0},{16,8},{24,16},{9,1},{17,9},{25,17},{10,2},{18,10},{26,18},{... | collective-permute-start | bytes 392 | tf_op jit(solution)/shard_map/ppermute | solution.py:30
  127.1 5.1 %collective-permute-start.7 = (f32[2,8,2]{2,0,1:T(2,128)S(1)}, f32[2,8,2]{2,0,1:T(2,128)S(1)}, u32[]{:S(2)}, u32[]{:S(2)}) collective-permute-start(f32[2,8,2]{2,0,1:T(2,128)S(1)} %get-tuple-element.175), channel_id=1, source_target_pairs={{0,1},{1,2},{2,3},{3,4},{4,5},{5,6},{6,7},{8,9},{9,10},{10,11},{11... | collective-permute-start | bytes 392 | tf_op jit(solution)/shard_map/ppermute | solution.py:29
  134.2 3.5 %collective-permute-done.8 = f32[2,8,2]{2,0,1:T(2,128)S(1)} collective-permute-done((f32[2,8,2]{2,0,1:T(2,128)S(1)}, f32[2,8,2]{2,0,1:T(2,128)S(1)}, u32[]{:S(2)}, u32[]{:S(2)}) %collective-permute-start.8) | collective-permute-done | bytes 160 | tf_op jit(solution)/shard_map/ppermute | solution.py:30
  138.7 6.2 %all-to-all-start = ((f32[8,2,4,8]{3,2,1,0:T(4,128)}), f32[8,2,4,8]{3,2,1,0:T(4,128)S(1)}, u32[]{:S(2)}, u32[]{:S(2)}) async-start(f32[8,2,4,8]{3,2,1,0:T(4,128)} %broadcast_in_dim.46), calls=%async_computation | async-start | bytes 65536 | tf_op jit(solution)/shard_map/all_to_all | solution.py:37
  144.9 4.2 %all-to-all-done = f32[8,2,4,8]{3,2,1,0:T(4,128)S(1)} async-done(((f32[8,2,4,8]{3,2,1,0:T(4,128)}), f32[8,2,4,8]{3,2,1,0:T(4,128)S(1)}, u32[]{:S(2)}, u32[]{:S(2)}) %all-to-all-start) | async-done | bytes 2080 | tf_op jit(solution)/shard_map/all_to_all | solution.py:37
  (109 shorter events, 67.8 us)
Async XLA Ops:
  0.6 26.4 %copy-start = (f32[1,256,512]{2,1,0:T(8,128)S(1)}, f32[1,256,512]{2,1,0:T(8,128)}, u32[]{:S(2)}) copy-start(f32[1,256,512]{2,1,0:T(8,128)} %param.3) | copy-start | bytes 1572868
  0.6 15.9 %collective-permute-start = (f32[256,512]{1,0:T(8,128)}, f32[256,512]{1,0:T(8,128)S(1)}, u32[]{:S(2)}, u32[]{:S(2)}) collective-permute-start(f32[256,512]{1,0:T(8,128)} %bitcast.162), channel_id=1, source_target_pairs={{32,0},{64,32},{96,64},{128,96},{160,128},{192,160},{224,192},{33,... | collective-permute-start | bytes 1572872 | tf_op jit(solution)/shard_map/ppermute | solution.py:19
  17.4 7.8 %collective-permute-start.1 = (f32[2,32,512]{2,1,0:T(8,128)S(1)}, f32[2,32,512]{2,1,0:T(8,128)S(1)}, u32[]{:S(2)}, u32[]{:S(2)}) collective-permute-start(f32[2,32,512]{2,1,0:T(8,128)S(1)} %get-tuple-element.173), channel_id=1, source_target_pairs={{0,8},{8,16},{16,24},{1,9},{9,17},{17,25},{2,10},{10,18},{18,26},{... | collective-permute-start | bytes 393224 | tf_op jit(solution)/shard_map/ppermute | solution.py:29
  19.4 7.7 %collective-permute-start.2 = (f32[2,32,512]{2,1,0:T(8,128)S(1)}, f32[2,32,512]{2,1,0:T(8,128)S(1)}, u32[]{:S(2)}, u32[]{:S(2)}) collective-permute-start(f32[2,32,512]{2,1,0:T(8,128)S(1)} %get-tuple-element.174), channel_id=1, source_target_pairs={{8,0},{16,8},{24,16},{9,1},{17,9},{25,17},{10,2},{18,10},{26,18},{... | collective-permute-start | bytes 393224 | tf_op jit(solution)/shard_map/ppermute | solution.py:30
  27.2 9.0 %collective-permute-start.3 = (f32[2,320,32]{2,1,0:T(8,128)S(1)}, f32[2,320,32]{2,1,0:T(8,128)S(1)}, u32[]{:S(2)}, u32[]{:S(2)}) collective-permute-start(f32[2,320,32]{2,1,0:T(8,128)S(1)} %get-tuple-element.171), channel_id=1, source_target_pairs={{0,1},{1,2},{2,3},{3,4},{4,5},{5,6},{6,7},{8,9},{9,10},{10,11},{11... | collective-permute-start | bytes 245768 | tf_op jit(solution)/shard_map/ppermute | solution.py:29
  31.0 10.1 %collective-permute-start.4 = (f32[2,320,32]{2,1,0:T(8,128)S(1)}, f32[2,320,32]{2,1,0:T(8,128)S(1)}, u32[]{:S(2)}, u32[]{:S(2)}) collective-permute-start(f32[2,320,32]{2,1,0:T(8,128)S(1)} %get-tuple-element.172), channel_id=1, source_target_pairs={{1,0},{2,1},{3,2},{4,3},{5,4},{6,5},{7,6},{9,8},{10,9},{11,10},{12... | collective-permute-start | bytes 245768 | tf_op jit(solution)/shard_map/ppermute | solution.py:30
  118.6 7.1 %collective-permute-start.5 = (f32[2,2,8]{2,0,1:T(2,128)S(1)}, f32[2,2,8]{2,0,1:T(2,128)S(1)}, u32[]{:S(2)}, u32[]{:S(2)}) collective-permute-start(f32[2,2,8]{2,0,1:T(2,128)S(1)} %get-tuple-element.179), channel_id=1, source_target_pairs={{0,8},{8,16},{16,24},{1,9},{9,17},{17,25},{2,10},{10,18},{18,26},{... | collective-permute-start | bytes 392 | tf_op jit(solution)/shard_map/ppermute | solution.py:29
  120.5 6.4 %collective-permute-start.6 = (f32[2,2,8]{2,0,1:T(2,128)S(1)}, f32[2,2,8]{2,0,1:T(2,128)S(1)}, u32[]{:S(2)}, u32[]{:S(2)}) collective-permute-start(f32[2,2,8]{2,0,1:T(2,128)S(1)} %get-tuple-element.180), channel_id=1, source_target_pairs={{8,0},{16,8},{24,16},{9,1},{17,9},{25,17},{10,2},{18,10},{26,18},{... | collective-permute-start | bytes 392 | tf_op jit(solution)/shard_map/ppermute | solution.py:30
  127.1 7.1 %collective-permute-start.7 = (f32[2,8,2]{2,0,1:T(2,128)S(1)}, f32[2,8,2]{2,0,1:T(2,128)S(1)}, u32[]{:S(2)}, u32[]{:S(2)}) collective-permute-start(f32[2,8,2]{2,0,1:T(2,128)S(1)} %get-tuple-element.175), channel_id=1, source_target_pairs={{0,1},{1,2},{2,3},{3,4},{4,5},{5,6},{6,7},{8,9},{9,10},{10,11},{11... | collective-permute-start | bytes 392 | tf_op jit(solution)/shard_map/ppermute | solution.py:29
  132.2 5.5 %collective-permute-start.8 = (f32[2,8,2]{2,0,1:T(2,128)S(1)}, f32[2,8,2]{2,0,1:T(2,128)S(1)}, u32[]{:S(2)}, u32[]{:S(2)}) collective-permute-start(f32[2,8,2]{2,0,1:T(2,128)S(1)} %get-tuple-element.176), channel_id=1, source_target_pairs={{1,0},{2,1},{3,2},{4,3},{5,4},{6,5},{7,6},{9,8},{10,9},{11,10},{12... | collective-permute-start | bytes 392 | tf_op jit(solution)/shard_map/ppermute | solution.py:30
  138.0 11.7 %copy-start.1 = (f32[2,4,8]{2,1,0:T(4,128)}, f32[2,4,8]{2,1,0:T(4,128)S(1)}, u32[]{:S(2)}) copy-start(f32[2,4,8]{2,1,0:T(4,128)S(1)} %copy.42) | copy-start | bytes 772
  138.7 10.4 %all-to-all-start = ((f32[8,2,4,8]{3,2,1,0:T(4,128)}), f32[8,2,4,8]{3,2,1,0:T(4,128)S(1)}, u32[]{:S(2)}, u32[]{:S(2)}) async-start(f32[8,2,4,8]{3,2,1,0:T(4,128)} %broadcast_in_dim.46), calls=%async_computation | async-start | bytes 65536 | tf_op jit(solution)/shard_map/all_to_all | solution.py:37
where the time goes:
time: 152 us; the launch traced here: 150 us
  matrix products  68.1 us (45%)
  starting transfers between devices  36.6 us (24%)
  waiting for transfers between devices  32 us (21%)
  other arithmetic  7.98 us (5%)
  local copies, waits for them, and re-layouts  3.73 us (2%)
    dot_general x24, matrix products, right_apply(): jnp.einsum('snjk,kl->snjl', values, table, precision=lax.Precision.HIGHEST)  40.4 us
    dot_general x24, matrix products, left_apply(): jnp.einsum('jk,snkl->snjl', table, values, precision=lax.Precision.HIGHEST)  27.7 us
    ppermute x4, starting transfers between devices, padded_2(): after = lax.ppermute(first, axis, down)  14.2 us
    ppermute x4, starting transfers between devices, padded_2(): before = lax.ppermute(last, axis, up)  12.8 us
    ppermute x1, waiting for transfers between devices, shifted(): return lax.ppermute(value, axis, pairs)  12.5 us
    ppermute x4, waiting for transfers between devices, padded_2(): after = lax.ppermute(first, axis, down)  11.5 us
    all_to_all x1, starting transfers between devices, from_everyone(): lax.all_to_all(jnp.broadcast_to(value[None], (length, *value.shape)), axi...  6.21 us
    all_to_all x1, waiting for transfers between devices, from_everyone(): lax.all_to_all(jnp.broadcast_to(value[None], (length, *value.shape)), axi...  4.19 us
  transfers between devices with their start and end apart: 10, of which 8 were waited for; matrix products, arithmetic and copies ran while one was open for 0% of the time, Pallas kernels for 0%

commit v1 on v0

v1 whole, which is shorter than its diff:
```python
import functools

import jax
import jax.numpy as jnp
import ml_dtypes
import numpy as np
from jax import lax
from jax.experimental import pallas as pl
from jax.experimental.pallas import tpu as pltpu
from jax.sharding import PartitionSpec as P

PATCH = 128
STRIDE = 64
HALF = 32
RATE = 0.25
GROUP = 4

MESH = pl.DeviceIdType.MESH
DIRECTIONS = [(dy, dx) for dy in (-1, 0, 1) for dx in (-1, 0, 1) if (dy, dx) != (0, 0)]
F32 = jnp.float32
BF16 = jnp.bfloat16


def split_table(table):
    high = table.astype(ml_dtypes.bfloat16)
    low = (table - high.astype(np.float64)).astype(ml_dtypes.bfloat16)
    return high, low


def tables():
    half = PATCH // 2
    point = np.arange(PATCH)
    angle = 2.0 * np.pi / PATCH
    packed = np.zeros((PATCH, PATCH))
    for k in range(half):
        packed[k] = np.cos(angle * (k * point % PATCH))
        packed[half + k] = np.sin(angle * (k * point % PATCH))
    packed[half] = np.cos(np.pi * point)
    weight = np.full(PATCH, 2.0)
    weight[0] = weight[half] = 1.0
    inverse = packed.T * weight[None, :] / PATCH

    def left(table):
        high, low = split_table(table)
        return np.block([[high, high], [low, low]])

    def right(table):
        high, low = split_table(table)
        return np.block([[high, low], [high, low]])

    scale = np.log2(np.e) / PATCH
    return np.stack(
        [right(packed.T), left(packed), left(inverse), right(inverse.T * scale)]
    ).astype(ml_dtypes.bfloat16)


def split(value):
    high = value.astype(BF16)
    low = (value - high.astype(F32)).astype(BF16)
    return high, low


def product(own, other):
    half = PATCH // 2
    lane = lax.broadcasted_iota(jnp.int32, (half, PATCH), 1)
    row = lax.broadcasted_iota(jnp.int32, (half, PATCH), 0)
    left = lane < half
    alone = (lane == 0) | (lane == half)
    plain = left | alone
    top_row = row == 0
    t, u = own[:half], own[half:]
    t2, u2 = other[:half], other[half:]
    rt2 = pltpu.roll(t2, half, 1)
    ru2 = pltpu.roll(u2, half, 1)
    uu, uru = u * u2, u * ru2
    g = t * t2 + jnp.where(top_row, 0.0, uu)
    h = t * rt2 + jnp.where(top_row, 0.0, uru)
    g2 = jnp.where(top_row, uu, t * u2 - u * t2)
    h2 = jnp.where(top_row, uru, t * ru2 - u * rt2)

    def joined(g, h):
        cross = pltpu.roll(jnp.where(left, h, g), half, 1)
        cross = jnp.where(alone, 0.0, cross)
        return jnp.where(plain, cross + g, cross - h)

    top = joined(g, h)
    top = jnp.where(top_row & (lane == 0), 0.0, top)
    return jnp.concatenate([top, joined(g2, h2)], axis=0)


def moments(scores):
    peak = jnp.max(jnp.max(scores, axis=0, keepdims=True), axis=1, keepdims=True)
    terms = jnp.exp2(scores - peak)
    total = None
    for g in range(PATCH // 8):
        part = terms[8 * g : 8 * g + 8]
        steps = float(g if g < PATCH // 16 else g - PATCH // 8)
        total = part if total is None else total + part
        first = part * steps if g == 0 else first + part * steps
    sub = lax.broadcasted_iota(jnp.int32, (8, PATCH), 0).astype(F32)
    lane = lax.broadcasted_iota(jnp.int32, (8, PATCH), 1)
    lag = jnp.where(lane < PATCH // 2, lane, lane - PATCH).astype(F32)
    return [
        jnp.sum(value, axis=0, keepdims=True)
        for value in (total, first * 8.0 + total * sub, total * lag)
    ]


def relax(flow, inside):
    def lap(value):
        return (
            pltpu.roll(value, 1, 0)
            + pltpu.roll(value, 7, 0)
            + pltpu.roll(value, 1, 1)
            + pltpu.roll(value, PATCH - 1, 1)
            - 4.0 * value
        )

    first = flow + RATE * (lap(flow) + flow - flow)
    first = jnp.where(inside, first, 0.0)
    return first + RATE * (lap(first) + flow - first)


def kernel(
    sizes, x_ref, tables_ref, out_ref, own, nxt, own_hi, own_lo, nxt_hi, nxt_lo, spec, table,
    stats, flows, around, meshes,
    local_sem, piece_send, piece_recv, own_send, own_recv, nxt_send, nxt_recv,
    flow_send, flow_recv, mesh_send, mesh_recv,
):
    n_sec, n_ty, n_tx = sizes
    rows, cols = x_ref.shape
    node_rows, node_cols = rows // STRIDE, cols // STRIDE
    wide = node_cols * PATCH
    sec, ty, tx = lax.axis_index("sec"), lax.axis_index("ty"), lax.axis_index("tx")

    def there(dy, dx):
        ok = jnp.bool_(True)
        if dy:
            ok = (ty + dy >= 0) & (ty + dy < n_ty)
        if dx:
            in_x = (tx + dx >= 0) & (tx + dx < n_tx)
            ok = ok & in_x if dy else in_x
        return ok

    has_next = sec < n_sec - 1
    has_before = sec > 0

    barrier = pltpu.get_barrier_semaphore()

    def greet(ok, s, y, x):
        @pl.when(ok)
        def _():
            pl.semaphore_signal(barrier, inc=1, device_id=(s, y, x), device_id_type=MESH)

    for dy, dx in DIRECTIONS:
        greet(there(dy, dx), sec, ty + dy, tx + dx)
    for d in range(1, n_sec):
        pl.semaphore_signal(
            barrier, inc=1, device_id=(lax.rem(sec + d, n_sec), ty, tx), device_id_type=MESH
        )

    tile = pltpu.make_async_copy(
        x_ref, own.at[pl.ds(HALF, rows), pl.ds(PATCH, cols)], local_sem.at[0]
    )
    tile.start()
    load = pltpu.make_async_copy(tables_ref, table, local_sem.at[1])
    load.start()

    for ref in (own, nxt):
        @pl.when(ty == 0)
        def _(ref=ref):
            ref[0:HALF, :] = jnp.zeros((HALF, cols + 2 * PATCH), F32)

        @pl.when(ty == n_ty - 1)
        def _(ref=ref):
            ref[HALF + rows : 2 * HALF + rows, :] = jnp.zeros((HALF, cols + 2 * PATCH), F32)

        @pl.when(tx == 0)
        def _(ref=ref):
            ref[:, 0:PATCH] = jnp.zeros((2 * HALF + rows, PATCH), F32)

        @pl.when(tx == n_tx - 1)
        def _(ref=ref):
            ref[:, PATCH + cols :] = jnp.zeros((2 * HALF + rows, PATCH), F32)

    for index, (dy, dx) in enumerate(DIRECTIONS):
        @pl.when(jnp.logical_not(there(-dy, -dx)))
        def _(index=index):
            around[index] = jnp.zeros((8, PATCH), F32)

    for t in range(n_sec):
        @pl.when(t >= sec)
        def _(t=t):
            meshes[t] = jnp.zeros((8, PATCH), F32)

    tall = 1 + (ty > 0).astype(jnp.int32) + (ty < n_ty - 1).astype(jnp.int32)
    broad = 1 + (tx > 0).astype(jnp.int32) + (tx < n_tx - 1).astype(jnp.int32)
    pl.semaphore_wait(barrier, n_sec - 1 + tall * broad - 1)

    inner_rows = rows - 2 * HALF
    mids = inner_rows // STRIDE
    pieces = [
        (0, HALF, 0, cols),
        (rows - HALF, HALF, 0, cols),
        (HALF, inner_rows, 0, PATCH),
        (HALF, inner_rows, cols - PATCH, PATCH),
    ]
    pieces += [(HALF + m * STRIDE, STRIDE, PATCH, cols - 2 * PATCH) for m in range(mids)]

    def piece_copy(p):
        r, nr, c, nc = pieces[p]
        return pltpu.make_async_remote_copy(
            src_ref=x_ref.at[pl.ds(r, nr), pl.ds(c, nc)],
            dst_ref=nxt.at[pl.ds(HALF + r, nr), pl.ds(PATCH + c, nc)],
            send_sem=piece_send.at[p],
            recv_sem=piece_recv.at[p],
            device_id=(sec - 1, ty, tx),
            device_id_type=MESH,
        )

    def border(axis_step, size, width):
        if axis_step == 0:
            return 0, size, 0
        if axis_step < 0:
            return 0, width, size
        return size - width, width, -width

    def border_copy(index, from_tile, target, send, recv):
        dy, dx = DIRECTIONS[index]
        r, nr, to_r = border(dy, rows, HALF)
        c, nc, to_c = border(dx, cols, PATCH)
        if from_tile:
            src = x_ref.at[pl.ds(r, nr), pl.ds(c, nc)]
        else:
            src = target.at[pl.ds(HALF + r, nr), pl.ds(PATCH + c, nc)]
        return pltpu.make_async_remote_copy(
            src_ref=src,
            dst_ref=target.at[pl.ds(HALF + to_r, nr), pl.ds(PATCH + to_c, nc)],
            send_sem=send.at[index],
            recv_sem=recv.at[index],
            device_id=(sec, ty + dy, tx + dx),
            device_id_type=MESH,
        )

    @pl.when(has_before)
    def _():
        for p in range(4):
            piece_copy(p).start()

    for index, (dy, dx) in enumerate(DIRECTIONS):
        @pl.when(there(dy, dx))
        def _(index=index):
            border_copy(index, True, own, own_send, own_recv).start()

    @pl.when(has_before)
    def _():
        for p in range(4, len(pieces)):
            piece_copy(p).start()

    lane = lax.broadcasted_iota(jnp.int32, (STRIDE, PATCH), 1)
    even, odd = lane < PATCH - HALF, lane >= HALF

    def right_chunk(source, high, low, b):
        at = pl.ds(pl.multiple_of(b * STRIDE, STRIDE), STRIDE)
        parts = []
        for j in range(node_cols):
            t = j // 2
            main = source[at, (t + 1) * PATCH : (t + 2) * PATCH]
            if j % 2 == 0:
                patch = jnp.where(even, main, source[at, t * PATCH : (t + 1) * PATCH])
            else:
                patch = jnp.where(odd, main, source[at, (t + 2) * PATCH : (t + 3) * PATCH])
            parts.append(jnp.concatenate(split(patch), axis=1))
        got = jnp.dot(jnp.concatenate(parts, axis=0), table[0], preferred_element_type=F32)
        got = got[:, :PATCH] + got[:, PATCH:]
        for j in range(node_cols):
            hi, lo = split(got[j * STRIDE : (j + 1) * STRIDE])
            high[at, j * PATCH : (j + 1) * PATCH] = hi
            low[at, j * PATCH : (j + 1) * PATCH] = lo

    def left_spectrum(high, low, i, columns):
        at = pl.ds(pl.multiple_of(i * STRIDE, STRIDE), PATCH)
        both = jnp.concatenate([high[at, columns], low[at, columns]], axis=0)
        got = jnp.dot(table[1], both, preferred_element_type=F32)
        return got[:PATCH] + got[PATCH:]

    tile.wait()
    load.wait()
    for index, (dy, dx) in enumerate(DIRECTIONS):
        @pl.when(there(-dy, -dx))
        def _(index=index):
            border_copy(index, True, own, own_send, own_recv).wait_recv()

    @pl.loop(0, node_rows + 1)
    def _(b):
        right_chunk(own, own_hi, own_lo, b)

    @pl.when(has_next)
    def _():
        for p in range(4):
            piece_copy(p).wait_recv()
        for index, (dy, dx) in enumerate(DIRECTIONS):
            @pl.when(there(dy, dx))
            def _(index=index):
                border_copy(index, False, nxt, nxt_send, nxt_recv).start()

    @pl.loop(0, node_rows)
    def _(i):
        for c in range(0, wide, 2 * PATCH):
            at = pl.ds(c, 2 * PATCH)
            spec[i, :, at] = left_spectrum(own_hi, own_lo, i, at)

    @pl.when(has_next)
    def _():
        for index, (dy, dx) in enumerate(DIRECTIONS):
            @pl.when(there(-dy, -dx))
            def _(index=index):
                border_copy(index, False, nxt, nxt_send, nxt_recv).wait_recv()

    right_chunk(nxt, nxt_hi, nxt_lo, 0)

    def mid_wait(m):
        at = pl.ds(pl.multiple_of(HALF + m * STRIDE, HALF), STRIDE)
        to = pl.ds(pl.multiple_of(2 * HALF + m * STRIDE, HALF), STRIDE)
        pltpu.make_async_remote_copy(
            src_ref=x_ref.at[at, pl.ds(PATCH, cols - 2 * PATCH)],
            dst_ref=nxt.at[to, pl.ds(2 * PATCH, cols - 2 * PATCH)],
            send_sem=piece_send.at[4 + m],
            recv_sem=piece_recv.at[4 + m],
            device_id=(sec - 1, ty, tx),
            device_id_type=MESH,
        ).wait_recv()

    @pl.loop(0, node_rows)
    def _(i):
        @pl.when(has_next & (i < mids))
        def _():
            mid_wait(i)

        right_chunk(nxt, nxt_hi, nxt_lo, i + 1)

        @pl.loop(0, node_cols // GROUP)
        def _(g):
            columns = pl.ds(pl.multiple_of(g * GROUP * PATCH, PATCH), GROUP * PATCH)
            other = left_spectrum(nxt_hi, nxt_lo, i, columns)
            mine = spec[i, :, columns]
            prods = jnp.concatenate(
                [
                    product(mine[:, n * PATCH : (n + 1) * PATCH], other[:, n * PATCH : (n + 1) * PATCH])
                    for n in range(GROUP)
                ],
                axis=1,
            )
            mixed = jnp.dot(
                table[2], jnp.concatenate(split(prods), axis=0), preferred_element_type=F32
            )
            hi, lo = split(mixed[:PATCH] + mixed[PATCH:])
            stacked = jnp.concatenate(
                [
                    jnp.concatenate(
                        [hi[:, n * PATCH : (n + 1) * PATCH], lo[:, n * PATCH : (n + 1) * PATCH]], axis=1
                    )
                    for n in range(GROUP)
                ],
                axis=0,
            )
            corr = jnp.dot(stacked, table[3], preferred_element_type=F32)
            corr = corr[:, :PATCH] + corr[:, PATCH:]
            found = [moments(corr[n * PATCH : (n + 1) * PATCH]) for n in range(GROUP)]
            for q in range(3):
                stats[q, i, pl.ds(g * GROUP, GROUP), :] = jnp.concatenate(
                    [f[q] for f in found], axis=0
                )

    lanes = lax.broadcasted_iota(jnp.int32, (8, PATCH), 1)
    columns = jnp.zeros((8, PATCH), F32)
    for i in range(node_rows):
        total, down, across = (jnp.sum(stats[q, i], axis=1, keepdims=True) for q in range(3))
        inv = 1.0 / total
        columns = jnp.where(lanes == i, down * inv, columns)
        columns = jnp.where(lanes == node_rows + i, across * inv, columns)
    columns = jnp.where(has_next, columns, 0.0)
    block = jnp.transpose(jnp.concatenate([columns] * 16, axis=0))[:8]
    flows[0] = block

    def flow_copy(index):
        dy, dx = DIRECTIONS[index]
        return pltpu.make_async_remote_copy(
            src_ref=flows.at[0],
            dst_ref=around.at[index],
            send_sem=flow_send.at[index],
            recv_sem=flow_recv.at[index],
            device_id=(sec, ty + dy, tx + dx),
            device_id_type=MESH,
        )

    for index, (dy, dx) in enumerate(DIRECTIONS):
        @pl.when(there(dy, dx))
        def _(index=index):
            flow_copy(index).start()
    for index, (dy, dx) in enumerate(DIRECTIONS):
        @pl.when(there(-dy, -dx))
        def _(index=index):
            flow_copy(index).wait_recv()

    lines = {}
    for dy in (-1, 0, 1):
        def from_(dx, dy=dy):
            return block if (dy, dx) == (0, 0) else around[DIRECTIONS.index((-dy, -dx))]

        line = jnp.where(lanes < 2 + node_cols, pltpu.roll(from_(0), 2, 1), pltpu.roll(from_(1), 2 + node_cols, 1))
        lines[dy] = jnp.where(lanes < 2, pltpu.roll(from_(-1), PATCH + 2 - node_cols, 1), line)

    subs = lax.broadcasted_iota(jnp.int32, (8, PATCH), 0)
    row_id = ty * node_rows + subs - 2
    col_id = tx * node_cols + lanes - 2
    inside = (
        (row_id >= 0) & (row_id < node_rows * n_ty) & (col_id >= 0) & (col_id < node_cols * n_tx)
    )
    done = []
    for c in range(2):
        base = c * node_rows
        above = pltpu.roll(lines[-1], (8 - (base + node_rows - 2)) % 8, 0)
        here = pltpu.roll(lines[0], (8 + 2 - base) % 8, 0)
        below = pltpu.roll(lines[1], (8 + 2 + node_rows - base) % 8, 0)
        flow = jnp.where(subs < 2, above, jnp.where(subs < 2 + node_rows, here, below))
        done.append(pltpu.roll(relax(flow, inside), PATCH - 2, 1))
    result = jnp.where(
        subs < node_rows, pltpu.roll(done[0], 6, 0), pltpu.roll(done[1], (8 + node_rows - 2) % 8, 0)
    )
    flows[1] = result

    def mesh_copy(d):
        return pltpu.make_async_remote_copy(
            src_ref=flows.at[1],
            dst_ref=meshes.at[sec],
            send_sem=mesh_send.at[d],
            recv_sem=mesh_recv.at[d],
            device_id=(sec + d, ty, tx),
            device_id_type=MESH,
        )

    def mesh_wait(d):
        pltpu.make_async_remote_copy(
            src_ref=flows.at[1],
            dst_ref=meshes.at[sec - d],
            send_sem=mesh_send.at[d],
            recv_sem=mesh_recv.at[d],
            device_id=(sec - d, ty, tx),
            device_id_type=MESH,
        ).wait_recv()

    for d in range(1, n_sec):
        @pl.when(sec + d < n_sec)
        def _(d=d):
            mesh_copy(d).start()
    for d in range(1, n_sec):
        @pl.when(sec - d >= 0)
        def _(d=d):
            mesh_wait(d)

    earlier = meshes[0]
    for t in range(1, n_sec):
        earlier = earlier + meshes[t]
    out_ref[0] = result
    out_ref[1] = earlier

    @pl.when(has_before)
    def _():
        for p in range(len(pieces)):
            piece_copy(p).wait_send()

    for index, (dy, dx) in enumerate(DIRECTIONS):
        @pl.when(there(dy, dx))
        def _(index=index):
            border_copy(index, True, own, own_send, own_recv).wait_send()
            flow_copy(index).wait_send()

            @pl.when(has_next)
            def _():
                border_copy(index, False, nxt, nxt_send, nxt_recv).wait_send()

    for d in range(1, n_sec):
        @pl.when(sec + d < n_sec)
        def _(d=d):
            mesh_copy(d).wait_send()


def solution(mesh):
    sizes = tuple(mesh.shape[axis] for axis in ("sec", "ty", "tx"))

    def on_device(images):
        image = images[0]
        rows, cols = image.shape
        node_rows, node_cols = rows // STRIDE, cols // STRIDE
        high = 2 * HALF + rows
        wide = node_cols * PATCH
        around = len(DIRECTIONS)
        n_pieces = 4 + (rows - 2 * HALF) // STRIDE
        dma = pltpu.SemaphoreType.DMA
        out = pl.pallas_call(
            functools.partial(kernel, sizes),
            out_shape=jax.ShapeDtypeStruct((2, 8, PATCH), F32),
            in_specs=[pl.BlockSpec(memory_space=pl.ANY)] * 2,
            out_specs=pl.BlockSpec(memory_space=pltpu.VMEM),
            scratch_shapes=[
                pltpu.VMEM((high, cols + 2 * PATCH), F32),
                pltpu.VMEM((high, cols + 2 * PATCH), F32),
                pltpu.VMEM((high, wide), BF16),
                pltpu.VMEM((high, wide), BF16),
                pltpu.VMEM((high, wide), BF16),
                pltpu.VMEM((high, wide), BF16),
                pltpu.VMEM((node_rows, PATCH, wide), F32),
                pltpu.VMEM((4, 2 * PATCH, 2 * PATCH), BF16),
                pltpu.VMEM((3, node_rows, node_cols, PATCH), F32),
                pltpu.VMEM((2, 8, PATCH), F32),
                pltpu.VMEM((around, 8, PATCH), F32),
                pltpu.VMEM((sizes[0], 8, PATCH), F32),
                dma((2,)),
                dma((n_pieces,)),
                dma((n_pieces,)),
                dma((around,)),
                dma((around,)),
                dma((around,)),
                dma((around,)),
                dma((around,)),
                dma((around,)),
                dma((sizes[0],)),
                dma((sizes[0],)),
            ],
            compiler_params=pltpu.CompilerParams(
                collective_id=0, has_side_effects=True, vmem_limit_bytes=40 * 1024 * 1024
            ),
        )(image, jnp.asarray(tables()))
        out = out[:, :, :node_cols].reshape(2, 1, 2, node_rows, node_cols)
        return out[0], out[1]

    return jax.shard_map(
        on_device,
        mesh=mesh,
        in_specs=(P("sec", "ty", "tx"),),
        out_specs=(P("sec", None, "ty", "tx"), P("sec", None, "ty", "tx")),
        check_vma=False,
    )
```

time: 152 us -> 44.6 us (0.29)
  the two profiles are of different devices: /device:TPU:92 before, /device:TPU:89 now
where the time goes in v1:
time: 44.6 us; the launch traced here: 44.5 us
  Pallas kernels  41.2 us (92%)
  local copies, waits for them, and re-layouts  2.68 us (6%)
  between operations  0.65 us (1%)
    pallas_call x1, Pallas kernels, on_device(): pl.pallas_call(functools.partial(kernel, sizes), out_shape=jax.ShapeDtype...  41.2 us
    unnamed x4, local copies, waits for them, and re-layouts  2.08 us

profile of v1, /device:TPU:89, one launch (start us, length us, event | category | flops | bytes accessed | tf_op | source)
XLA Modules:
  0.0 44.5 jit_solution(5589094413593417597)
XLA Ops:
  0.6 0.0 copy-start
  0.6 1.0 %copy-done = f32[1,256,512]{2,1,0:T(8,128)S(1)} copy-done((f32[1,256,512]{2,1,0:T(8,128)S(1)}, f32[1,256,512]{2,1,0:T(8,128)}, u32[]{:S(2)}) %copy-start) | copy-done | bytes 524312
  1.7 0.0 copy-start.1
  1.7 1.0 %copy-done.1 = bf16[4,256,256]{2,1,0:T(8,128)(2,1)S(1)} copy-done((bf16[4,256,256]{2,1,0:T(8,128)(2,1)S(1)}, bf16[4,256,256]{2,1,0:T(8,128)(2,1)}, u32[]{:S(2)}) %copy-start.1) | copy-done | bytes 524312
  2.7 41.2 %shard_map.41 = f32[2,8,128]{2,1,0:T(8,128)S(1)} custom-call(f32[256,512]{1,0:T(8,128)S(1)} %bitcast.3, bf16[4,256,256]{2,1,0:T(8,128)(2,1)S(1)} %copy-done.1), custom_call_target="tpu_custom_call" | custom-call | tf_op jit(solution)/shard_map/pallas_call | solution.py:501
  43.9 0.6 %fusion = (f32[1,8,8]{2,1,0:T(8,128)}, f32[1,8,8]{2,1,0:T(8,128)}) fusion(f32[2,8,128]{2,1,0:T(8,128)S(1)} %shard_map.41), kind=kLoop, calls=%fused_computation | loop fusion | bytes 1024 | tf_op jit(solution)/shard_map/slice | solution.py:536
Async XLA Ops:
  0.6 1.0 %copy-start = (f32[1,256,512]{2,1,0:T(8,128)S(1)}, f32[1,256,512]{2,1,0:T(8,128)}, u32[]{:S(2)}) copy-start(f32[1,256,512]{2,1,0:T(8,128)} %param.2) | copy-start | bytes 1572868
  1.7 1.0 %copy-start.1 = (bf16[4,256,256]{2,1,0:T(8,128)(2,1)S(1)}, bf16[4,256,256]{2,1,0:T(8,128)(2,1)}, u32[]{:S(2)}) copy-start(bf16[4,256,256]{2,1,0:T(8,128)(2,1)} %constant.2.clone.tables_ref) | copy-start | bytes 1572868

commit v2 on v1

--- a/solution.py
+++ b/solution.py
@@ -13,7 +13,6 @@
 STRIDE = 64
 HALF = 32
 RATE = 0.25
-GROUP = 4
 
 MESH = pl.DeviceIdType.MESH
 DIRECTIONS = [(dy, dx) for dy in (-1, 0, 1) for dx in (-1, 0, 1) if (dy, dx) != (0, 0)]
@@ -124,7 +123,8 @@
 def kernel(
     sizes, x_ref, tables_ref, out_ref, own, nxt, own_hi, own_lo, nxt_hi, nxt_lo, spec, table,
     stats, flows, around, meshes,
-    local_sem, piece_send, piece_recv, own_send, own_recv, nxt_send, nxt_recv,
+    own_pack, own_land, nxt_pack, nxt_land,
+    local_sem, piece_send, piece_recv, own_send, own_recv, nxt_send, nxt_recv, straight_send,
     flow_send, flow_recv, mesh_send, mesh_recv,
 ):
     n_sec, n_ty, n_tx = sizes
@@ -145,6 +145,12 @@
     has_next = sec < n_sec - 1
     has_before = sec > 0
 
+    def crosses(dy):
+        return (ty % 2 == 1) if dy > 0 else (ty % 2 == 0)
+
+    def straight(dy, dx):
+        return crosses(dy) & there(dy, dx)
+
     barrier = pltpu.get_barrier_semaphore()
 
     def greet(ok, s, y, x):
@@ -154,6 +160,10 @@
 
     for dy, dx in DIRECTIONS:
         greet(there(dy, dx), sec, ty + dy, tx + dx)
+    for dy in (-1, 1):
+        for dx in (-1, 0, 1):
+            greet(has_before & straight(dy, dx), sec - 1, ty + dy, tx + dx)
+            greet(has_next & straight(dy, dx), sec + 1, ty + dy, tx + dx)
     for d in range(1, n_sec):
         pl.semaphore_signal(
             barrier, inc=1, device_id=(lax.rem(sec + d, n_sec), ty, tx), device_id_type=MESH
@@ -195,7 +205,9 @@
 
     tall = 1 + (ty > 0).astype(jnp.int32) + (ty < n_ty - 1).astype(jnp.int32)
     broad = 1 + (tx > 0).astype(jnp.int32) + (tx < n_tx - 1).astype(jnp.int32)
-    pl.semaphore_wait(barrier, n_sec - 1 + tall * broad - 1)
+    apart = (crosses(-1) & there(-1, 0)).astype(jnp.int32) + (crosses(1) & there(1, 0)).astype(jnp.int32)
+    ends = has_before.astype(jnp.int32) + has_next.astype(jnp.int32)
+    pl.semaphore_wait(barrier, n_sec - 1 + tall * broad - 1 + apart * broad * ends)
 
     inner_rows = rows - 2 * HALF
     mids = inner_rows // STRIDE
@@ -225,37 +237,93 @@
             return 0, width, size
         return size - width, width, -width
 
-    def border_copy(index, from_tile, target, send, recv):
+    def border_copy(index, source, target, send, recv, to_sec, pack=None, land=None):
         dy, dx = DIRECTIONS[index]
-        r, nr, to_r = border(dy, rows, HALF)
-        c, nc, to_c = border(dx, cols, PATCH)
-        if from_tile:
-            src = x_ref.at[pl.ds(r, nr), pl.ds(c, nc)]
+        if dy == 0:
+            side = (dx + 1) // 2
+            src, dst = pack.at[side], land.at[side]
         else:
-            src = target.at[pl.ds(HALF + r, nr), pl.ds(PATCH + c, nc)]
+            r, nr, to_r = border(dy, rows, HALF)
+            c, nc, to_c = border(dx, cols, PATCH)
+            if source is None:
+                src = x_ref.at[pl.ds(r, nr), pl.ds(c, nc)]
+            else:
+                src = source.at[pl.ds(HALF + r, nr), pl.ds(PATCH + c, nc)]
+            dst = target.at[pl.ds(HALF + to_r, nr), pl.ds(PATCH + to_c, nc)]
         return pltpu.make_async_remote_copy(
             src_ref=src,
-            dst_ref=target.at[pl.ds(HALF + to_r, nr), pl.ds(PATCH + to_c, nc)],
+            dst_ref=dst,
             send_sem=send.at[index],
             recv_sem=recv.at[index],
-            device_id=(sec, ty + dy, tx + dx),
+            device_id=(to_sec, ty + dy, tx + dx),
             device_id_type=MESH,
         )
+
+    def own_border(index):
+        return border_copy(index, None, own, own_send, own_recv, sec, own_pack, own_land)
+
+    def nxt_border(index):
+        return border_copy(index, nxt, nxt, nxt_send, nxt_recv, sec, nxt_pack, nxt_land)
+
+    def nxt_straight(index):
+        return border_copy(index, None, nxt, straight_send, nxt_recv, sec - 1)
+
+    UPDOWN = [k for k, (dy, dx) in enumerate(DIRECTIONS) if dy]
+    SIDES = [k for k, (dy, dx) in enumerate(DIRECTIONS) if not dy]
+
+    def each(indices, ok, do):
+        for index in indices:
+            @pl.when(ok(*DIRECTIONS[index]))
+            def _(index=index):
+                do(index)
+
+    def from_there(dy, dx):
+        return there(-dy, -dx)
+
+    def handed_on(dy, dx):
+        return jnp.logical_not(crosses(dy)) & there(dy, dx)
+
+    span = rows // 4
+    packed_lane = lax.broadcasted_iota(jnp.int32, (span, PATCH), 1)
+
+    def pack_columns(source, into):
+        for side, at in enumerate((PATCH, cols)):
+            first = 0 if side == 0 else PATCH - HALF
+            value = None
+            for q in range(4):
+                part = source[HALF + span * q : HALF + span * (q + 1), at : at + PATCH]
+                part = pltpu.roll(part, (HALF * q - first) % PATCH, 1) if HALF * q != first else part
+                value = part if q == 0 else jnp.where(packed_lane >= HALF * q, part, value)
+            into[side] = value
+
+    def unpack_columns(land, target):
+        for side, at in enumerate((PATCH + cols, 0)):
+            first = 0 if side == 0 else PATCH - HALF
+
+            @pl.when(there(0, 1 - 2 * side))
+            def _(side=side, at=at, first=first):
+                for q in range(4):
+                    part = land[side]
+                    part = pltpu.roll(part, (first - HALF * q) % PATCH, 1) if HALF * q != first else part
+                    target[HALF + span * q : HALF + span * (q + 1), at : at + PATCH] = part
 
     @pl.when(has_before)
     def _():
         for p in range(4):
             piece_copy(p).start()
-
-    for index, (dy, dx) in enumerate(DIRECTIONS):
-        @pl.when(there(dy, dx))
-        def _(index=index):
-            border_copy(index, True, own, own_send, own_recv).start()
+        each(UPDOWN, straight, lambda k: nxt_straight(k).start())
+
+    each(UPDOWN, there, lambda k: own_border(k).start())
 
     @pl.when(has_before)
     def _():
         for p in range(4, len(pieces)):
             piece_copy(p).start()
+
+    tile.wait()
+    pack_columns(own, own_pack)
+    each(SIDES, there, lambda k: own_border(k).start())
+    load.wait()
 
     lane = lax.broadcasted_iota(jnp.int32, (STRIDE, PATCH), 1)
     even, odd = lane < PATCH - HALF, lane >= HALF
@@ -284,12 +352,8 @@
         got = jnp.dot(table[1], both, preferred_element_type=F32)
         return got[:PATCH] + got[PATCH:]
 
-    tile.wait()
-    load.wait()
-    for index, (dy, dx) in enumerate(DIRECTIONS):
-        @pl.when(there(-dy, -dx))
-        def _(index=index):
-            border_copy(index, True, own, own_send, own_recv).wait_recv()
+    each(range(len(DIRECTIONS)), from_there, lambda k: own_border(k).wait_recv())
+    unpack_columns(own_land, own)
 
     @pl.loop(0, node_rows + 1)
     def _(b):
@@ -297,12 +361,9 @@
 
     @pl.when(has_next)
     def _():
-        for p in range(4):
-            piece_copy(p).wait_recv()
-        for index, (dy, dx) in enumerate(DIRECTIONS):
-            @pl.when(there(dy, dx))
-            def _(index=index):
-                border_copy(index, False, nxt, nxt_send, nxt_recv).start()
+        piece_copy(0).wait_recv()
+        piece_copy(1).wait_recv()
+        each(UPDOWN, handed_on, lambda k: nxt_border(k).start())
 
     @pl.loop(0, node_rows)
     def _(i):
@@ -312,12 +373,15 @@
 
     @pl.when(has_next)
     def _():
-        for index, (dy, dx) in enumerate(DIRECTIONS):
-            @pl.when(there(-dy, -dx))
-            def _(index=index):
-                border_copy(index, False, nxt, nxt_send, nxt_recv).wait_recv()
+        piece_copy(2).wait_recv()
+        piece_copy(3).wait_recv()
+        pack_columns(nxt, nxt_pack)
+        each(SIDES, there, lambda k: nxt_border(k).start())
+        each(range(len(DIRECTIONS)), from_there, lambda k: nxt_border(k).wait_recv())
+        unpack_columns(nxt_land, nxt)
 
     right_chunk(nxt, nxt_hi, nxt_lo, 0)
+    right_chunk(nxt, nxt_hi, nxt_lo, node_rows)
 
     def mid_wait(m):
         at = pl.ds(pl.multiple_of(HALF + m * STRIDE, HALF), STRIDE)
@@ -333,44 +397,30 @@
 
     @pl.loop(0, node_rows)
     def _(i):
-        @pl.when(has_next & (i < mids))
+        @pl.when(i < mids)
         def _():
-            mid_wait(i)
-
-        right_chunk(nxt, nxt_hi, nxt_lo, i + 1)
-
-        @pl.loop(0, node_cols // GROUP)
-        def _(g):
-            columns = pl.ds(pl.multiple_of(g * GROUP * PATCH, PATCH), GROUP * PATCH)
-            other = left_spectrum(nxt_hi, nxt_lo, i, columns)
-            mine = spec[i, :, columns]
-            prods = jnp.concatenate(
-                [
-                    product(mine[:, n * PATCH : (n + 1) * PATCH], other[:, n * PATCH : (n + 1) * PATCH])
-                    for n in range(GROUP)
-                ],
-                axis=1,
-            )
-            mixed = jnp.dot(
-                table[2], jnp.concatenate(split(prods), axis=0), preferred_element_type=F32
-            )
-            hi, lo = split(mixed[:PATCH] + mixed[PATCH:])
-            stacked = jnp.concatenate(
-                [
-                    jnp.concatenate(
-                        [hi[:, n * PATCH : (n + 1) * PATCH], lo[:, n * PATCH : (n + 1) * PATCH]], axis=1
-                    )
-                    for n in range(GROUP)
-                ],
-                axis=0,
-            )
-            corr = jnp.dot(stacked, table[3], preferred_element_type=F32)
-            corr = corr[:, :PATCH] + corr[:, PATCH:]
-            found = [moments(corr[n * PATCH : (n + 1) * PATCH]) for n in range(GROUP)]
-            for q in range(3):
-                stats[q, i, pl.ds(g * GROUP, GROUP), :] = jnp.concatenate(
-                    [f[q] for f in found], axis=0
-                )
+            @pl.when(has_next)
+            def _():
+                mid_wait(i)
+
+            right_chunk(nxt, nxt_hi, nxt_lo, i + 1)
+
+        nodes = [slice(n * PATCH, (n + 1) * PATCH) for n in range(node_cols)]
+        other = left_spectrum(nxt_hi, nxt_lo, i, pl.ds(0, wide))
+        mine = spec[i]
+        prods = jnp.concatenate([product(mine[:, n], other[:, n]) for n in nodes], axis=1)
+        mixed = jnp.dot(
+            table[2], jnp.concatenate(split(prods), axis=0), preferred_element_type=F32
+        )
+        hi, lo = split(mixed[:PATCH] + mixed[PATCH:])
+        stacked = jnp.concatenate(
+            [jnp.concatenate([hi[:, n], lo[:, n]], axis=1) for n in nodes], axis=0
+        )
+        corr = jnp.dot(stacked, table[3], preferred_element_type=F32)
+        corr = corr[:, :PATCH] + corr[:, PATCH:]
+        found = [moments(corr[n]) for n in nodes]
+        for q in range(3):
+            stats[q, i] = jnp.concatenate([f[q] for f in found], axis=0)
 
     lanes = lax.broadcasted_iota(jnp.int32, (8, PATCH), 1)
     columns = jnp.zeros((8, PATCH), F32)
@@ -470,15 +520,18 @@
         for p in range(len(pieces)):
             piece_copy(p).wait_send()
 
-    for index, (dy, dx) in enumerate(DIRECTIONS):
-        @pl.when(there(dy, dx))
-        def _(index=index):
-            border_copy(index, True, own, own_send, own_recv).wait_send()
-            flow_copy(index).wait_send()
-
-            @pl.when(has_next)
-            def _():
-                border_copy(index, False, nxt, nxt_send, nxt_recv).wait_send()
+    every = range(len(DIRECTIONS))
+    each(every, there, lambda k: own_border(k).wait_send())
+    each(every, there, lambda k: flow_copy(k).wait_send())
+
+    @pl.when(has_before)
+    def _():
+        each(UPDOWN, straight, lambda k: nxt_straight(k).wait_send())
+
+    @pl.when(has_next)
+    def _():
+        each(UPDOWN, handed_on, lambda k: nxt_border(k).wait_send())
+        each(SIDES, there, lambda k: nxt_border(k).wait_send())
 
     for d in range(1, n_sec):
         @pl.when(sec + d < n_sec)
@@ -516,9 +569,14 @@
                 pltpu.VMEM((2, 8, PATCH), F32),
                 pltpu.VMEM((around, 8, PATCH), F32),
                 pltpu.VMEM((sizes[0], 8, PATCH), F32),
+                pltpu.VMEM((2, rows // 4, PATCH), F32),
+                pltpu.VMEM((2, rows // 4, PATCH), F32),
+                pltpu.VMEM((2, rows // 4, PATCH), F32),
+                pltpu.VMEM((2, rows // 4, PATCH), F32),
                 dma((2,)),
                 dma((n_pieces,)),
                 dma((n_pieces,)),
+                dma((around,)),
                 dma((around,)),
                 dma((around,)),
                 dma((around,)),
@@ -529,7 +587,7 @@
                 dma((sizes[0],)),
             ],
             compiler_params=pltpu.CompilerParams(
-                collective_id=0, has_side_effects=True, vmem_limit_bytes=40 * 1024 * 1024
+                collective_id=0, has_side_effects=True, vmem_limit_bytes=60 * 1024 * 1024
             ),
         )(image, jnp.asarray(tables()))
         out = out[:, :, :node_cols].reshape(2, 1, 2, node_rows, node_cols)

time: 44.6 us -> 40.9 us (0.917)
  the two profiles are of different devices: /device:TPU:89 before, /device:TPU:59 now
where the time goes in v2:
time: 40.9 us; the launch traced here: 40.8 us
  Pallas kernels  38.9 us (95%)
  local copies, waits for them, and re-layouts  1.28 us (3%)
  between operations  0.64 us (2%)
    pallas_call x1, Pallas kernels, on_device(): pl.pallas_call(functools.partial(kernel, sizes), out_shape=jax.ShapeDtype...  38.9 us
    slice x1, local copies, waits for them, and re-layouts, on_device(): return (out[0], out[1])  1.28 us

profile of v2, /device:TPU:59, one launch (start us, length us, event | category | flops | bytes accessed | tf_op | source)
XLA Modules:
  0.0 40.8 jit_solution(4824239012904892332)
XLA Ops:
  0.6 38.9 %shard_map.41 = f32[2,8,128]{2,1,0:T(8,128)} custom-call(f32[256,512]{1,0:T(8,128)} %bitcast.3, bf16[4,256,256]{2,1,0:T(8,128)(2,1)} %constant.2.clone.tables_ref), custom_call_target="tpu_custom_call" | custom-call | tf_op jit(solution)/shard_map/pallas_call | solution.py:554
  39.5 1.3 %fusion = (f32[1,8,8]{2,1,0:T(8,128)}, f32[1,8,8]{2,1,0:T(8,128)}) fusion(f32[2,8,128]{2,1,0:T(8,128)} %shard_map.41), kind=kLoop, calls=%fused_computation | loop fusion | bytes 1024 | tf_op jit(solution)/shard_map/slice | solution.py:594

commit v3 on v2

--- a/solution.py
+++ b/solution.py
@@ -148,8 +148,8 @@
     def crosses(dy):
         return (ty % 2 == 1) if dy > 0 else (ty % 2 == 0)
 
-    def straight(dy, dx):
-        return crosses(dy) & there(dy, dx)
+    def straight(dy):
+        return crosses(dy) & there(dy, 0)
 
     barrier = pltpu.get_barrier_semaphore()
 
@@ -161,9 +161,8 @@
     for dy, dx in DIRECTIONS:
         greet(there(dy, dx), sec, ty + dy, tx + dx)
     for dy in (-1, 1):
-        for dx in (-1, 0, 1):
-            greet(has_before & straight(dy, dx), sec - 1, ty + dy, tx + dx)
-            greet(has_next & straight(dy, dx), sec + 1, ty + dy, tx + dx)
+        greet(has_before & straight(dy), sec - 1, ty + dy, tx)
+        greet(has_next & straight(dy), sec + 1, ty + dy, tx)
     for d in range(1, n_sec):
         pl.semaphore_signal(
             barrier, inc=1, device_id=(lax.rem(sec + d, n_sec), ty, tx), device_id_type=MESH
@@ -207,83 +206,95 @@
     broad = 1 + (tx > 0).astype(jnp.int32) + (tx < n_tx - 1).astype(jnp.int32)
     apart = (crosses(-1) & there(-1, 0)).astype(jnp.int32) + (crosses(1) & there(1, 0)).astype(jnp.int32)
     ends = has_before.astype(jnp.int32) + has_next.astype(jnp.int32)
-    pl.semaphore_wait(barrier, n_sec - 1 + tall * broad - 1 + apart * broad * ends)
-
-    inner_rows = rows - 2 * HALF
-    mids = inner_rows // STRIDE
-    pieces = [
-        (0, HALF, 0, cols),
-        (rows - HALF, HALF, 0, cols),
-        (HALF, inner_rows, 0, PATCH),
-        (HALF, inner_rows, cols - PATCH, PATCH),
-    ]
-    pieces += [(HALF + m * STRIDE, STRIDE, PATCH, cols - 2 * PATCH) for m in range(mids)]
+    pl.semaphore_wait(barrier, n_sec - 1 + tall * broad - 1 + apart * ends)
+
+    pieces = [(0, HALF), (rows - HALF, HALF), None]
+    pieces += [(r, HALF) for r in range(HALF, rows - HALF, HALF)]
+    inner = 3
 
     def piece_copy(p):
-        r, nr, c, nc = pieces[p]
+        if p == 2:
+            src, dst = own_pack, nxt_pack
+        else:
+            r, nr = pieces[p]
+            src = x_ref.at[pl.ds(r, nr)]
+            dst = nxt.at[pl.ds(HALF + r, nr), pl.ds(PATCH, cols)]
         return pltpu.make_async_remote_copy(
-            src_ref=x_ref.at[pl.ds(r, nr), pl.ds(c, nc)],
-            dst_ref=nxt.at[pl.ds(HALF + r, nr), pl.ds(PATCH + c, nc)],
+            src_ref=src,
+            dst_ref=dst,
             send_sem=piece_send.at[p],
             recv_sem=piece_recv.at[p],
             device_id=(sec - 1, ty, tx),
             device_id_type=MESH,
         )
 
-    def border(axis_step, size, width):
-        if axis_step == 0:
-            return 0, size, 0
-        if axis_step < 0:
-            return 0, width, size
-        return size - width, width, -width
-
-    def border_copy(index, source, target, send, recv, to_sec, pack=None, land=None):
-        dy, dx = DIRECTIONS[index]
-        if dy == 0:
-            side = (dx + 1) // 2
-            src, dst = pack.at[side], land.at[side]
+    def advance(p):
+        @pl.when(has_before)
+        def _():
+            piece_copy(p).wait_send()
+            piece_copy(p + 2).start()
+
+    def edge(dy):
+        return (0, HALF + rows) if dy < 0 else (rows - HALF, 0)
+
+    def row_copy(dy, through, target, send, recv, to_sec):
+        r, to = edge(dy)
+        if through is None:
+            src = x_ref.at[pl.ds(r, HALF)]
         else:
-            r, nr, to_r = border(dy, rows, HALF)
-            c, nc, to_c = border(dx, cols, PATCH)
-            if source is None:
-                src = x_ref.at[pl.ds(r, nr), pl.ds(c, nc)]
-            else:
-                src = source.at[pl.ds(HALF + r, nr), pl.ds(PATCH + c, nc)]
-            dst = target.at[pl.ds(HALF + to_r, nr), pl.ds(PATCH + to_c, nc)]
+            src = through.at[pl.ds(HALF + r, HALF), pl.ds(PATCH, cols)]
+        side = (dy + 1) // 2
         return pltpu.make_async_remote_copy(
             src_ref=src,
-            dst_ref=dst,
-            send_sem=send.at[index],
-            recv_sem=recv.at[index],
-            device_id=(to_sec, ty + dy, tx + dx),
+            dst_ref=target.at[pl.ds(to, HALF), pl.ds(PATCH, cols)],
+            send_sem=send.at[side],
+            recv_sem=recv.at[side],
+            device_id=(to_sec, ty + dy, tx),
             device_id_type=MESH,
         )
 
-    def own_border(index):
-        return border_copy(index, None, own, own_send, own_recv, sec, own_pack, own_land)
-
-    def nxt_border(index):
-        return border_copy(index, nxt, nxt, nxt_send, nxt_recv, sec, nxt_pack, nxt_land)
-
-    def nxt_straight(index):
-        return border_copy(index, None, nxt, straight_send, nxt_recv, sec - 1)
-
-    UPDOWN = [k for k, (dy, dx) in enumerate(DIRECTIONS) if dy]
-    SIDES = [k for k, (dy, dx) in enumerate(DIRECTIONS) if not dy]
-
-    def each(indices, ok, do):
-        for index in indices:
-            @pl.when(ok(*DIRECTIONS[index]))
-            def _(index=index):
-                do(index)
-
-    def from_there(dy, dx):
-        return there(-dy, -dx)
-
-    def handed_on(dy, dx):
-        return jnp.logical_not(crosses(dy)) & there(dy, dx)
-
-    span = rows // 4
+    def column_copy(dx, pack, land, send, recv):
+        side = (dx + 1) // 2
+        return pltpu.make_async_remote_copy(
+            src_ref=pack.at[side],
+            dst_ref=land.at[side],
+            send_sem=send.at[2 + side],
+            recv_sem=recv.at[2 + side],
+            device_id=(sec, ty, tx + dx),
+            device_id_type=MESH,
+        )
+
+    def own_rows(dy):
+        return row_copy(dy, None, own, own_send, own_recv, sec)
+
+    def own_columns(dx):
+        return column_copy(dx, own_pack, own_land, own_send, own_recv)
+
+    def nxt_rows(dy):
+        return row_copy(dy, nxt, nxt, nxt_send, nxt_recv, sec)
+
+    def nxt_straight(dy):
+        return row_copy(dy, None, nxt, straight_send, nxt_recv, sec - 1)
+
+    def nxt_columns(dx):
+        return column_copy(dx, nxt_pack, nxt_land, nxt_send, nxt_recv)
+
+    def up_down(ok, do):
+        for dy in (-1, 1):
+            @pl.when(ok(dy))
+            def _(dy=dy):
+                do(dy)
+
+    def sides(sign, do):
+        for dx in (-1, 1):
+            @pl.when(there(0, sign * dx))
+            def _(dx=dx):
+                do(dx)
+
+    def handed_on(dy):
+        return jnp.logical_not(crosses(dy)) & there(dy, 0)
+
+    span = (rows + 2 * HALF) // 4
     packed_lane = lax.broadcasted_iota(jnp.int32, (span, PATCH), 1)
 
     def pack_columns(source, into):
@@ -291,7 +302,7 @@
             first = 0 if side == 0 else PATCH - HALF
             value = None
             for q in range(4):
-                part = source[HALF + span * q : HALF + span * (q + 1), at : at + PATCH]
+                part = source[span * q : span * (q + 1), at : at + PATCH]
                 part = pltpu.roll(part, (HALF * q - first) % PATCH, 1) if HALF * q != first else part
                 value = part if q == 0 else jnp.where(packed_lane >= HALF * q, part, value)
             into[side] = value
@@ -305,24 +316,21 @@
                 for q in range(4):
                     part = land[side]
                     part = pltpu.roll(part, (first - HALF * q) % PATCH, 1) if HALF * q != first else part
-                    target[HALF + span * q : HALF + span * (q + 1), at : at + PATCH] = part
+                    target[span * q : span * (q + 1), at : at + PATCH] = part
+
+    up_down(lambda dy: there(dy, 0), lambda dy: own_rows(dy).start())
 
     @pl.when(has_before)
     def _():
-        for p in range(4):
-            piece_copy(p).start()
-        each(UPDOWN, straight, lambda k: nxt_straight(k).start())
-
-    each(UPDOWN, there, lambda k: own_border(k).start())
-
-    @pl.when(has_before)
-    def _():
-        for p in range(4, len(pieces)):
-            piece_copy(p).start()
+        piece_copy(0).start()
+        piece_copy(1).start()
+        up_down(straight, lambda dy: nxt_straight(dy).start())
 
     tile.wait()
+    up_down(lambda dy: there(-dy, 0), lambda dy: own_rows(dy).wait_recv())
     pack_columns(own, own_pack)
-    each(SIDES, there, lambda k: own_border(k).start())
+    sides(1, lambda dx: own_columns(dx).start())
+    advance(0)
     load.wait()
 
     lane = lax.broadcasted_iota(jnp.int32, (STRIDE, PATCH), 1)
@@ -352,18 +360,27 @@
         got = jnp.dot(table[1], both, preferred_element_type=F32)
         return got[:PATCH] + got[PATCH:]
 
-    each(range(len(DIRECTIONS)), from_there, lambda k: own_border(k).wait_recv())
-    unpack_columns(own_land, own)
-
-    @pl.loop(0, node_rows + 1)
-    def _(b):
-        right_chunk(own, own_hi, own_lo, b)
+    advance(1)
 
     @pl.when(has_next)
     def _():
         piece_copy(0).wait_recv()
         piece_copy(1).wait_recv()
-        each(UPDOWN, handed_on, lambda k: nxt_border(k).start())
+        up_down(handed_on, lambda dy: nxt_rows(dy).start())
+
+    sides(-1, lambda dx: own_columns(dx).wait_recv())
+    unpack_columns(own_land, own)
+
+    @pl.loop(0, node_rows + 1)
+    def _(b):
+        right_chunk(own, own_hi, own_lo, b)
+
+    advance(2)
+
+    @pl.when(has_next)
+    def _():
+        piece_copy(2).wait_recv()
+        sides(1, lambda dx: nxt_columns(dx).start())
 
     @pl.loop(0, node_rows)
     def _(i):
@@ -371,37 +388,38 @@
             at = pl.ds(c, 2 * PATCH)
             spec[i, :, at] = left_spectrum(own_hi, own_lo, i, at)
 
+    advance(3)
+
     @pl.when(has_next)
     def _():
-        piece_copy(2).wait_recv()
-        piece_copy(3).wait_recv()
-        pack_columns(nxt, nxt_pack)
-        each(SIDES, there, lambda k: nxt_border(k).start())
-        each(range(len(DIRECTIONS)), from_there, lambda k: nxt_border(k).wait_recv())
+        up_down(lambda dy: there(-dy, 0), lambda dy: nxt_rows(dy).wait_recv())
+        sides(-1, lambda dx: nxt_columns(dx).wait_recv())
         unpack_columns(nxt_land, nxt)
 
     right_chunk(nxt, nxt_hi, nxt_lo, 0)
     right_chunk(nxt, nxt_hi, nxt_lo, node_rows)
-
-    def mid_wait(m):
-        at = pl.ds(pl.multiple_of(HALF + m * STRIDE, HALF), STRIDE)
-        to = pl.ds(pl.multiple_of(2 * HALF + m * STRIDE, HALF), STRIDE)
+    advance(4)
+
+    def inner_wait(m):
+        at = pl.ds(pl.multiple_of(HALF + m * HALF, HALF), HALF)
+        to = pl.ds(pl.multiple_of(2 * HALF + m * HALF, HALF), HALF)
         pltpu.make_async_remote_copy(
-            src_ref=x_ref.at[at, pl.ds(PATCH, cols - 2 * PATCH)],
-            dst_ref=nxt.at[to, pl.ds(2 * PATCH, cols - 2 * PATCH)],
-            send_sem=piece_send.at[4 + m],
-            recv_sem=piece_recv.at[4 + m],
+            src_ref=x_ref.at[at],
+            dst_ref=nxt.at[to, pl.ds(PATCH, cols)],
+            send_sem=piece_send.at[inner + m],
+            recv_sem=piece_recv.at[inner + m],
             device_id=(sec - 1, ty, tx),
             device_id_type=MESH,
         ).wait_recv()
 
     @pl.loop(0, node_rows)
     def _(i):
-        @pl.when(i < mids)
+        @pl.when(i < node_rows - 1)
         def _():
             @pl.when(has_next)
             def _():
-                mid_wait(i)
+                inner_wait(2 * i)
+                inner_wait(2 * i + 1)
 
             right_chunk(nxt, nxt_hi, nxt_lo, i + 1)
 
@@ -421,6 +439,11 @@
         found = [moments(corr[n]) for n in nodes]
         for q in range(3):
             stats[q, i] = jnp.concatenate([f[q] for f in found], axis=0)
+
+        @pl.when(i == 0)
+        def _():
+            for p in range(5, len(pieces) - 2):
+                advance(p)
 
     lanes = lax.broadcasted_iota(jnp.int32, (8, PATCH), 1)
     columns = jnp.zeros((8, PATCH), F32)
@@ -515,23 +538,24 @@
     out_ref[0] = result
     out_ref[1] = earlier
 
+    for index, (dy, dx) in enumerate(DIRECTIONS):
+        @pl.when(there(dy, dx))
+        def _(index=index):
+            flow_copy(index).wait_send()
+
+    up_down(lambda dy: there(dy, 0), lambda dy: own_rows(dy).wait_send())
+    sides(1, lambda dx: own_columns(dx).wait_send())
+
     @pl.when(has_before)
     def _():
-        for p in range(len(pieces)):
+        for p in range(len(pieces) - 2, len(pieces)):
             piece_copy(p).wait_send()
-
-    every = range(len(DIRECTIONS))
-    each(every, there, lambda k: own_border(k).wait_send())
-    each(every, there, lambda k: flow_copy(k).wait_send())
-
-    @pl.when(has_before)
-    def _():
-        each(UPDOWN, straight, lambda k: nxt_straight(k).wait_send())
+        up_down(straight, lambda dy: nxt_straight(dy).wait_send())
 
     @pl.when(has_next)
     def _():
-        each(UPDOWN, handed_on, lambda k: nxt_border(k).wait_send())
-        each(SIDES, there, lambda k: nxt_border(k).wait_send())
+        up_down(handed_on, lambda dy: nxt_rows(dy).wait_send())
+        sides(1, lambda dx: nxt_columns(dx).wait_send())
 
     for d in range(1, n_sec):
         @pl.when(sec + d < n_sec)
@@ -549,7 +573,7 @@
         high = 2 * HALF + rows
         wide = node_cols * PATCH
         around = len(DIRECTIONS)
-        n_pieces = 4 + (rows - 2 * HALF) // STRIDE
+        n_pieces = 3 + (rows - 2 * HALF) // HALF
         dma = pltpu.SemaphoreType.DMA
         out = pl.pallas_call(
             functools.partial(kernel, sizes),
@@ -569,18 +593,18 @@
                 pltpu.VMEM((2, 8, PATCH), F32),
                 pltpu.VMEM((around, 8, PATCH), F32),
                 pltpu.VMEM((sizes[0], 8, PATCH), F32),
-                pltpu.VMEM((2, rows // 4, PATCH), F32),
-                pltpu.VMEM((2, rows // 4, PATCH), F32),
-                pltpu.VMEM((2, rows // 4, PATCH), F32),
-                pltpu.VMEM((2, rows // 4, PATCH), F32),
+                pltpu.VMEM((2, high // 4, PATCH), F32),
+                pltpu.VMEM((2, high // 4, PATCH), F32),
+                pltpu.VMEM((2, high // 4, PATCH), F32),
+                pltpu.VMEM((2, high // 4, PATCH), F32),
                 dma((2,)),
                 dma((n_pieces,)),
                 dma((n_pieces,)),
-                dma((around,)),
-                dma((around,)),
-                dma((around,)),
-                dma((around,)),
-                dma((around,)),
+                dma((4,)),
+                dma((4,)),
+                dma((4,)),
+                dma((4,)),
+                dma((2,)),
                 dma((around,)),
                 dma((around,)),
                 dma((sizes[0],)),

time: 40.9 us -> 38.7 us (0.946)
  the two profiles are of different devices: /device:TPU:59 before, /device:TPU:25 now
where the time goes in v3:
time: 38.7 us; the launch traced here: 38.6 us
  Pallas kernels  36.7 us (95%)
  local copies, waits for them, and re-layouts  1.28 us (3%)
  between operations  0.64 us (2%)
    pallas_call x1, Pallas kernels, on_device(): pl.pallas_call(functools.partial(kernel, sizes), out_shape=jax.ShapeDtype...  36.7 us
    slice x1, local copies, waits for them, and re-layouts, on_device(): return (out[0], out[1])  1.28 us

profile of v3, /device:TPU:25, one launch (start us, length us, event | category | flops | bytes accessed | tf_op | source)
XLA Modules:
  0.0 38.6 jit_solution(12888266269073237386)
XLA Ops:
  0.6 36.7 %shard_map.41 = f32[2,8,128]{2,1,0:T(8,128)} custom-call(f32[256,512]{1,0:T(8,128)} %bitcast.3, bf16[4,256,256]{2,1,0:T(8,128)(2,1)} %constant.2.clone.tables_ref), custom_call_target="tpu_custom_call" | custom-call | tf_op jit(solution)/shard_map/pallas_call | solution.py:578
  37.3 1.3 %fusion = (f32[1,8,8]{2,1,0:T(8,128)}, f32[1,8,8]{2,1,0:T(8,128)}) fusion(f32[2,8,128]{2,1,0:T(8,128)} %shard_map.41), kind=kLoop, calls=%fused_computation | loop fusion | bytes 1024 | tf_op jit(solution)/shard_map/slice | solution.py:618

commit v4 on v3

--- a/solution.py
+++ b/solution.py
@@ -208,17 +208,25 @@
     ends = has_before.astype(jnp.int32) + has_next.astype(jnp.int32)
     pl.semaphore_wait(barrier, n_sec - 1 + tall * broad - 1 + apart * ends)
 
-    pieces = [(0, HALF), (rows - HALF, HALF), None]
-    pieces += [(r, HALF) for r in range(HALF, rows - HALF, HALF)]
-    inner = 3
+    middle = rows // 2 - HALF
+    pieces = [
+        (0, HALF, 0, cols),
+        (rows - HALF, HALF, 0, cols),
+        None,
+        (HALF, STRIDE, 0, cols),
+        (rows - HALF - STRIDE, STRIDE, 0, cols),
+        (middle, STRIDE, 0, 2 * PATCH),
+        (middle, STRIDE, 3 * PATCH, PATCH),
+        (middle, STRIDE, 2 * PATCH, PATCH),
+    ]
 
     def piece_copy(p):
         if p == 2:
             src, dst = own_pack, nxt_pack
         else:
-            r, nr = pieces[p]
-            src = x_ref.at[pl.ds(r, nr)]
-            dst = nxt.at[pl.ds(HALF + r, nr), pl.ds(PATCH, cols)]
+            r, nr, c, nc = pieces[p]
+            src = x_ref.at[pl.ds(r, nr), pl.ds(c, nc)]
+            dst = nxt.at[pl.ds(HALF + r, nr), pl.ds(PATCH + c, nc)]
         return pltpu.make_async_remote_copy(
             src_ref=src,
             dst_ref=dst,
@@ -228,11 +236,11 @@
             device_id_type=MESH,
         )
 
-    def advance(p):
-        @pl.when(has_before)
+    def arrived(*indices):
+        @pl.when(has_next)
         def _():
-            piece_copy(p).wait_send()
-            piece_copy(p + 2).start()
+            for p in indices:
+                piece_copy(p).wait_recv()
 
     def edge(dy):
         return (0, HALF + rows) if dy < 0 else (rows - HALF, 0)
@@ -330,29 +338,39 @@
     up_down(lambda dy: there(-dy, 0), lambda dy: own_rows(dy).wait_recv())
     pack_columns(own, own_pack)
     sides(1, lambda dx: own_columns(dx).start())
-    advance(0)
+
+    @pl.when(has_before)
+    def _():
+        for p in range(2, len(pieces)):
+            piece_copy(p).start()
+
     load.wait()
 
     lane = lax.broadcasted_iota(jnp.int32, (STRIDE, PATCH), 1)
     even, odd = lane < PATCH - HALF, lane >= HALF
 
-    def right_chunk(source, high, low, b):
-        at = pl.ds(pl.multiple_of(b * STRIDE, STRIDE), STRIDE)
-        parts = []
-        for j in range(node_cols):
+    order = [node_cols - 1, *range(node_cols - 1)]
+    part_cols = node_cols // 2
+    parts = (range(0, part_cols), range(part_cols, node_cols))
+    every = range(node_cols)
+
+    def right_chunk(source, high, low, b, places):
+        at = pl.ds(b * STRIDE if isinstance(b, int) else pl.multiple_of(b * STRIDE, STRIDE), STRIDE)
+        patches = []
+        for j in (order[p] for p in places):
             t = j // 2
             main = source[at, (t + 1) * PATCH : (t + 2) * PATCH]
             if j % 2 == 0:
                 patch = jnp.where(even, main, source[at, t * PATCH : (t + 1) * PATCH])
             else:
                 patch = jnp.where(odd, main, source[at, (t + 2) * PATCH : (t + 3) * PATCH])
-            parts.append(jnp.concatenate(split(patch), axis=1))
-        got = jnp.dot(jnp.concatenate(parts, axis=0), table[0], preferred_element_type=F32)
+            patches.append(jnp.concatenate(split(patch), axis=1))
+        got = jnp.dot(jnp.concatenate(patches, axis=0), table[0], preferred_element_type=F32)
         got = got[:, :PATCH] + got[:, PATCH:]
-        for j in range(node_cols):
-            hi, lo = split(got[j * STRIDE : (j + 1) * STRIDE])
-            high[at, j * PATCH : (j + 1) * PATCH] = hi
-            low[at, j * PATCH : (j + 1) * PATCH] = lo
+        for n, p in enumerate(places):
+            hi, lo = split(got[n * STRIDE : (n + 1) * STRIDE])
+            high[at, p * PATCH : (p + 1) * PATCH] = hi
+            low[at, p * PATCH : (p + 1) * PATCH] = lo
 
     def left_spectrum(high, low, i, columns):
         at = pl.ds(pl.multiple_of(i * STRIDE, STRIDE), PATCH)
@@ -360,7 +378,6 @@
         got = jnp.dot(table[1], both, preferred_element_type=F32)
         return got[:PATCH] + got[PATCH:]
 
-    advance(1)
 
     @pl.when(has_next)
     def _():
@@ -373,9 +390,8 @@
 
     @pl.loop(0, node_rows + 1)
     def _(b):
-        right_chunk(own, own_hi, own_lo, b)
-
-    advance(2)
+        right_chunk(own, own_hi, own_lo, b, every)
+
 
     @pl.when(has_next)
     def _():
@@ -388,7 +404,6 @@
             at = pl.ds(c, 2 * PATCH)
             spec[i, :, at] = left_spectrum(own_hi, own_lo, i, at)
 
-    advance(3)
 
     @pl.when(has_next)
     def _():
@@ -396,70 +411,25 @@
         sides(-1, lambda dx: nxt_columns(dx).wait_recv())
         unpack_columns(nxt_land, nxt)
 
-    right_chunk(nxt, nxt_hi, nxt_lo, 0)
-    right_chunk(nxt, nxt_hi, nxt_lo, node_rows)
-    advance(4)
-
-    def inner_wait(m):
-        at = pl.ds(pl.multiple_of(HALF + m * HALF, HALF), HALF)
-        to = pl.ds(pl.multiple_of(2 * HALF + m * HALF, HALF), HALF)
-        pltpu.make_async_remote_copy(
-            src_ref=x_ref.at[at],
-            dst_ref=nxt.at[to, pl.ds(PATCH, cols)],
-            send_sem=piece_send.at[inner + m],
-            recv_sem=piece_recv.at[inner + m],
-            device_id=(sec - 1, ty, tx),
-            device_id_type=MESH,
-        ).wait_recv()
-
-    @pl.loop(0, node_rows)
-    def _(i):
-        @pl.when(i < node_rows - 1)
-        def _():
-            @pl.when(has_next)
-            def _():
-                inner_wait(2 * i)
-                inner_wait(2 * i + 1)
-
-            right_chunk(nxt, nxt_hi, nxt_lo, i + 1)
-
-        nodes = [slice(n * PATCH, (n + 1) * PATCH) for n in range(node_cols)]
-        other = left_spectrum(nxt_hi, nxt_lo, i, pl.ds(0, wide))
-        mine = spec[i]
-        prods = jnp.concatenate([product(mine[:, n], other[:, n]) for n in nodes], axis=1)
-        mixed = jnp.dot(
-            table[2], jnp.concatenate(split(prods), axis=0), preferred_element_type=F32
-        )
-        hi, lo = split(mixed[:PATCH] + mixed[PATCH:])
-        stacked = jnp.concatenate(
-            [jnp.concatenate([hi[:, n], lo[:, n]], axis=1) for n in nodes], axis=0
-        )
-        corr = jnp.dot(stacked, table[3], preferred_element_type=F32)
-        corr = corr[:, :PATCH] + corr[:, PATCH:]
-        found = [moments(corr[n]) for n in nodes]
-        for q in range(3):
-            stats[q, i] = jnp.concatenate([f[q] for f in found], axis=0)
-
-        @pl.when(i == 0)
-        def _():
-            for p in range(5, len(pieces) - 2):
-                advance(p)
+    right_chunk(nxt, nxt_hi, nxt_lo, 0, every)
+    right_chunk(nxt, nxt_hi, nxt_lo, node_rows, every)
 
     lanes = lax.broadcasted_iota(jnp.int32, (8, PATCH), 1)
-    columns = jnp.zeros((8, PATCH), F32)
-    for i in range(node_rows):
-        total, down, across = (jnp.sum(stats[q, i], axis=1, keepdims=True) for q in range(3))
-        inv = 1.0 / total
-        columns = jnp.where(lanes == i, down * inv, columns)
-        columns = jnp.where(lanes == node_rows + i, across * inv, columns)
-    columns = jnp.where(has_next, columns, 0.0)
-    block = jnp.transpose(jnp.concatenate([columns] * 16, axis=0))[:8]
-    flows[0] = block
+
+    def flow_block(indices):
+        columns = jnp.zeros((8, PATCH), F32)
+        for i in indices:
+            total, down, across = (jnp.sum(stats[q, i], axis=1, keepdims=True) for q in range(3))
+            inv = 1.0 / total
+            columns = jnp.where(lanes == i, down * inv, columns)
+            columns = jnp.where(lanes == node_rows + i, across * inv, columns)
+        columns = pltpu.roll(jnp.where(has_next, columns, 0.0), node_cols - 1, 0)
+        return jnp.transpose(jnp.concatenate([columns] * 16, axis=0))[:8]
 
     def flow_copy(index):
         dy, dx = DIRECTIONS[index]
         return pltpu.make_async_remote_copy(
-            src_ref=flows.at[0],
+            src_ref=flows.at[1 if dy and dx else 0],
             dst_ref=around.at[index],
             send_sem=flow_send.at[index],
             recv_sem=flow_recv.at[index],
@@ -467,14 +437,85 @@
             device_id_type=MESH,
         )
 
-    for index, (dy, dx) in enumerate(DIRECTIONS):
-        @pl.when(there(dy, dx))
-        def _(index=index):
-            flow_copy(index).start()
-    for index, (dy, dx) in enumerate(DIRECTIONS):
-        @pl.when(there(-dy, -dx))
-        def _(index=index):
-            flow_copy(index).wait_recv()
+    def flow_each(sign, corners, do):
+        for index, (dy, dx) in enumerate(DIRECTIONS):
+            if bool(dy and dx) in corners:
+                @pl.when(there(sign * dy, sign * dx))
+                def _(index=index):
+                    do(index)
+
+    last = node_rows - 1
+
+    @pl.loop(0, 4)
+    def _(step):
+        @pl.when(step == 0)
+        def _():
+            arrived(3)
+            right_chunk(nxt, nxt_hi, nxt_lo, 1, every)
+
+        @pl.when(step == 1)
+        def _():
+            arrived(4)
+            right_chunk(nxt, nxt_hi, nxt_lo, last, every)
+
+        @pl.when(step == 2)
+        def _():
+            flows[1] = flow_block((0, last))
+            flow_each(1, (True,), lambda k: flow_copy(k).start())
+            arrived(5, 6)
+            right_chunk(nxt, nxt_hi, nxt_lo, 2, parts[0])
+
+        @pl.when(step == 3)
+        def _():
+            arrived(7)
+            right_chunk(nxt, nxt_hi, nxt_lo, 2, parts[1])
+
+        halves = [
+            (jnp.where(step < 2, step * last, 1 + h), jnp.where(step < 2, h, step - 2)) for h in range(2)
+        ]
+        nodes = [slice(n * PATCH, (n + 1) * PATCH) for n in range(node_cols)]
+        mine, other = [], []
+        for i, g in halves:
+            columns = pl.ds(pl.multiple_of(g * part_cols * PATCH, PATCH), part_cols * PATCH)
+            other.append(left_spectrum(nxt_hi, nxt_lo, i, columns))
+            mine.append(spec[i, :, columns])
+        mine, other = (jnp.concatenate(value, axis=1) for value in (mine, other))
+        prods = jnp.concatenate([product(mine[:, n], other[:, n]) for n in nodes], axis=1)
+        mixed = jnp.dot(
+            table[2], jnp.concatenate(split(prods), axis=0), preferred_element_type=F32
+        )
+        hi, lo = split(mixed[:PATCH] + mixed[PATCH:])
+        stacked = jnp.concatenate(
+            [jnp.concatenate([hi[:, n], lo[:, n]], axis=1) for n in nodes], axis=0
+        )
+        corr = jnp.dot(stacked, table[3], preferred_element_type=F32)
+        corr = corr[:, :PATCH] + corr[:, PATCH:]
+        found = [moments(corr[n]) for n in nodes]
+        for h, (i, g) in enumerate(halves):
+            for q in range(3):
+                stats[q, i, pl.ds(g * part_cols, part_cols), :] = jnp.concatenate(
+                    [f[q] for f in found[h * part_cols : (h + 1) * part_cols]], axis=0
+                )
+
+    block = flow_block(range(node_rows))
+    flows[0] = block
+    flow_each(1, (False,), lambda k: flow_copy(k).start())
+
+    up_down(lambda dy: there(dy, 0), lambda dy: own_rows(dy).wait_send())
+    sides(1, lambda dx: own_columns(dx).wait_send())
+
+    @pl.when(has_before)
+    def _():
+        for p in range(len(pieces)):
+            piece_copy(p).wait_send()
+        up_down(straight, lambda dy: nxt_straight(dy).wait_send())
+
+    @pl.when(has_next)
+    def _():
+        up_down(handed_on, lambda dy: nxt_rows(dy).wait_send())
+        sides(1, lambda dx: nxt_columns(dx).wait_send())
+
+    flow_each(-1, (True, False), lambda k: flow_copy(k).wait_recv())
 
     lines = {}
     for dy in (-1, 0, 1):
@@ -501,11 +542,11 @@
     result = jnp.where(
         subs < node_rows, pltpu.roll(done[0], 6, 0), pltpu.roll(done[1], (8 + node_rows - 2) % 8, 0)
     )
-    flows[1] = result
+    flows[2] = result
 
     def mesh_copy(d):
         return pltpu.make_async_remote_copy(
-            src_ref=flows.at[1],
+            src_ref=flows.at[2],
             dst_ref=meshes.at[sec],
             send_sem=mesh_send.at[d],
             recv_sem=mesh_recv.at[d],
@@ -515,7 +556,7 @@
 
     def mesh_wait(d):
         pltpu.make_async_remote_copy(
-            src_ref=flows.at[1],
+            src_ref=flows.at[2],
             dst_ref=meshes.at[sec - d],
             send_sem=mesh_send.at[d],
             recv_sem=mesh_recv.at[d],
@@ -538,25 +579,7 @@
     out_ref[0] = result
     out_ref[1] = earlier
 
-    for index, (dy, dx) in enumerate(DIRECTIONS):
-        @pl.when(there(dy, dx))
-        def _(index=index):
-            flow_copy(index).wait_send()
-
-    up_down(lambda dy: there(dy, 0), lambda dy: own_rows(dy).wait_send())
-    sides(1, lambda dx: own_columns(dx).wait_send())
-
-    @pl.when(has_before)
-    def _():
-        for p in range(len(pieces) - 2, len(pieces)):
-            piece_copy(p).wait_send()
-        up_down(straight, lambda dy: nxt_straight(dy).wait_send())
-
-    @pl.when(has_next)
-    def _():
-        up_down(handed_on, lambda dy: nxt_rows(dy).wait_send())
-        sides(1, lambda dx: nxt_columns(dx).wait_send())
-
+    flow_each(1, (True, False), lambda k: flow_copy(k).wait_send())
     for d in range(1, n_sec):
         @pl.when(sec + d < n_sec)
         def _(d=d):
@@ -573,7 +596,7 @@
         high = 2 * HALF + rows
         wide = node_cols * PATCH
         around = len(DIRECTIONS)
-        n_pieces = 3 + (rows - 2 * HALF) // HALF
+        n_pieces = 8
         dma = pltpu.SemaphoreType.DMA
         out = pl.pallas_call(
             functools.partial(kernel, sizes),
@@ -590,7 +613,7 @@
                 pltpu.VMEM((node_rows, PATCH, wide), F32),
                 pltpu.VMEM((4, 2 * PATCH, 2 * PATCH), BF16),
                 pltpu.VMEM((3, node_rows, node_cols, PATCH), F32),
-                pltpu.VMEM((2, 8, PATCH), F32),
+                pltpu.VMEM((3, 8, PATCH), F32),
                 pltpu.VMEM((around, 8, PATCH), F32),
                 pltpu.VMEM((sizes[0], 8, PATCH), F32),
                 pltpu.VMEM((2, high // 4, PATCH), F32),

time: 38.7 us -> 34.8 us (0.90)
  the two profiles are of different devices: /device:TPU:25 before, /device:TPU:28 now
where the time goes in v4:
time: 34.8 us; the launch traced here: 34.7 us
  Pallas kernels  32.8 us (94%)
  local copies, waits for them, and re-layouts  1.28 us (4%)
  between operations  0.64 us (2%)
    pallas_call x1, Pallas kernels, on_device(): pl.pallas_call(functools.partial(kernel, sizes), out_shape=jax.ShapeDtype...  32.8 us
    slice x1, local copies, waits for them, and re-layouts, on_device(): return (out[0], out[1])  1.28 us

profile of v4, /device:TPU:28, one launch (start us, length us, event | category | flops | bytes accessed | tf_op | source)
XLA Modules:
  0.0 34.7 jit_solution(657528497011846693)
XLA Ops:
  0.6 32.8 %shard_map.41 = f32[2,8,128]{2,1,0:T(8,128)} custom-call(f32[256,512]{1,0:T(8,128)} %bitcast.3, bf16[4,256,256]{2,1,0:T(8,128)(2,1)} %constant.2.clone.tables_ref), custom_call_target="tpu_custom_call" | custom-call | tf_op jit(solution)/shard_map/pallas_call | solution.py:601
  33.4 1.3 %fusion = (f32[1,8,8]{2,1,0:T(8,128)}, f32[1,8,8]{2,1,0:T(8,128)}) fusion(f32[2,8,128]{2,1,0:T(8,128)} %shard_map.41), kind=kLoop, calls=%fused_computation | loop fusion | bytes 1024 | tf_op jit(solution)/shard_map/slice | solution.py:641

commit v5 on v4

--- a/solution.py
+++ b/solution.py
@@ -15,6 +15,7 @@
 RATE = 0.25
 
 MESH = pl.DeviceIdType.MESH
+CORNERS = [(dy, dx) for dy in (-1, 1) for dx in (-1, 1)]
 DIRECTIONS = [(dy, dx) for dy in (-1, 0, 1) for dx in (-1, 0, 1) if (dy, dx) != (0, 0)]
 F32 = jnp.float32
 BF16 = jnp.bfloat16
@@ -123,8 +124,9 @@
 def kernel(
     sizes, x_ref, tables_ref, out_ref, own, nxt, own_hi, own_lo, nxt_hi, nxt_lo, spec, table,
     stats, flows, around, meshes,
-    own_pack, own_land, nxt_pack, nxt_land,
+    own_pack, own_land, nxt_pack, nxt_land, own_rest, nxt_rest, tips, own_tips, nxt_tips,
     local_sem, piece_send, piece_recv, own_send, own_recv, nxt_send, nxt_recv, straight_send,
+    tip_send, own_tip_recv, nxt_tip_recv,
     flow_send, flow_recv, mesh_send, mesh_recv,
 ):
     n_sec, n_ty, n_tx = sizes
@@ -163,6 +165,9 @@
     for dy in (-1, 1):
         greet(has_before & straight(dy), sec - 1, ty + dy, tx)
         greet(has_next & straight(dy), sec + 1, ty + dy, tx)
+    for dy, dx in CORNERS:
+        greet(has_before & there(dy, dx), sec - 1, ty + dy, tx + dx)
+        greet(has_next & there(dy, dx), sec + 1, ty + dy, tx + dx)
     for d in range(1, n_sec):
         pl.semaphore_signal(
             barrier, inc=1, device_id=(lax.rem(sec + d, n_sec), ty, tx), device_id_type=MESH
@@ -202,29 +207,100 @@
         def _(t=t):
             meshes[t] = jnp.zeros((8, PATCH), F32)
 
+    span = rows // 4
+    spans = [(HALF + span * q, span) for q in range(4)]
+
+    def turned(value, by):
+        return pltpu.roll(value, by % PATCH, 1) if by % PATCH else value
+
+    def packed(source, where, side):
+        lane = lax.broadcasted_iota(jnp.int32, (where[0][1], PATCH), 1)
+        at, first = ((PATCH, 0), (cols, PATCH - HALF))[side]
+        value = None
+        for q, (r, nr) in enumerate(where):
+            part = turned(source[r : r + nr, at : at + PATCH], HALF * q - first)
+            value = part if q == 0 else jnp.where(lane >= HALF * q, part, value)
+        return value
+
+    def unpack(value, target, where, side):
+        at, first = ((PATCH + cols, 0), (0, PATCH - HALF))[side]
+        for q, (r, nr) in enumerate(where):
+            target[r : r + nr, at : at + PATCH] = turned(value, first - HALF * q)
+
+    def unpack_columns(land, target):
+        for side in range(2):
+            @pl.when(there(0, 1 - 2 * side))
+            def _(side=side):
+                unpack(land[side], target, spans, side)
+
+    def eighths(start):
+        return [(start + 8 * q, 8) for q in range(4)]
+
+    def unpack_tip(land, target, k):
+        dy, dx = CORNERS[k]
+        unpack(land[k], target, eighths(HALF + rows if dy < 0 else 0), (dx + 1) // 2)
+
+    def pack_rest(m):
+        lane = lax.broadcasted_iota(jnp.int32, (STRIDE, PATCH), 1)
+        r = 2 * HALF + m * STRIDE
+        left = own[r : r + STRIDE, PATCH : 2 * PATCH]
+        right = own[r : r + STRIDE, cols : cols + PATCH]
+        own_rest[m, 0:STRIDE] = jnp.where(lane < PATCH - HALF, right, left)
+        own_rest[m, STRIDE : STRIDE + HALF] = jnp.where(
+            lane[:HALF] < STRIDE, turned(left[:HALF], -HALF), turned(left[HALF:], HALF)
+        )
+
+    def unpack_rest(m):
+        lane = lax.broadcasted_iota(jnp.int32, (HALF, PATCH), 1)
+        for h in range(2):
+            r = HALF + m * STRIDE + h * HALF
+            q, start = r // span, r % span
+            border = [nxt_pack[side, start : start + HALF] for side in range(2)]
+            main = nxt_rest[m, h * HALF : (h + 1) * HALF]
+            half = turned(nxt_rest[m, STRIDE : STRIDE + HALF], HALF if h == 0 else -HALF)
+            left = jnp.where(lane < PATCH - HALF, half, main)
+            left = jnp.where(lane < HALF, turned(border[0], -HALF * q), left)
+            right = jnp.where(lane < PATCH - HALF, main, turned(border[1], PATCH - HALF - HALF * q))
+            nxt[HALF + r : 2 * HALF + r, PATCH : 2 * PATCH] = left
+            nxt[HALF + r : 2 * HALF + r, cols : cols + PATCH] = right
+
+    tile.wait()
+    for side in range(2):
+        own_pack[side] = packed(own, spans, side)
+    for k, (dy, dx) in enumerate(CORNERS):
+        tips[k] = packed(own, eighths(HALF if dy < 0 else rows), (dx + 1) // 2)
+    for m in range((rows - 2 * HALF) // STRIDE):
+        pack_rest(m)
+
     tall = 1 + (ty > 0).astype(jnp.int32) + (ty < n_ty - 1).astype(jnp.int32)
     broad = 1 + (tx > 0).astype(jnp.int32) + (tx < n_tx - 1).astype(jnp.int32)
     apart = (crosses(-1) & there(-1, 0)).astype(jnp.int32) + (crosses(1) & there(1, 0)).astype(jnp.int32)
     ends = has_before.astype(jnp.int32) + has_next.astype(jnp.int32)
-    pl.semaphore_wait(barrier, n_sec - 1 + tall * broad - 1 + apart * ends)
-
-    middle = rows // 2 - HALF
+    pl.semaphore_wait(barrier, n_sec - 1 + tall * broad - 1 + (apart + (tall - 1) * (broad - 1)) * ends)
+
+    bands = (rows - 2 * HALF) // STRIDE
+    middle = bands // 2
     pieces = [
         (0, HALF, 0, cols),
         (rows - HALF, HALF, 0, cols),
         None,
-        (HALF, STRIDE, 0, cols),
-        (rows - HALF - STRIDE, STRIDE, 0, cols),
-        (middle, STRIDE, 0, 2 * PATCH),
-        (middle, STRIDE, 3 * PATCH, PATCH),
-        (middle, STRIDE, 2 * PATCH, PATCH),
+        0,
+        (HALF, STRIDE, PATCH, 2 * PATCH),
+        bands - 1,
+        (rows - HALF - STRIDE, STRIDE, PATCH, 2 * PATCH),
+        middle,
+        (HALF + middle * STRIDE, STRIDE, PATCH, PATCH),
+        (HALF + middle * STRIDE, STRIDE, 2 * PATCH, PATCH),
     ]
 
     def piece_copy(p):
-        if p == 2:
+        piece = pieces[p]
+        if piece is None:
             src, dst = own_pack, nxt_pack
+        elif isinstance(piece, int):
+            src, dst = own_rest.at[piece], nxt_rest.at[piece]
         else:
-            r, nr, c, nc = pieces[p]
+            r, nr, c, nc = piece
             src = x_ref.at[pl.ds(r, nr), pl.ds(c, nc)]
             dst = nxt.at[pl.ds(HALF + r, nr), pl.ds(PATCH + c, nc)]
         return pltpu.make_async_remote_copy(
@@ -287,6 +363,23 @@
     def nxt_columns(dx):
         return column_copy(dx, nxt_pack, nxt_land, nxt_send, nxt_recv)
 
+    def tip_copy(k, section):
+        dy, dx = CORNERS[k]
+        return pltpu.make_async_remote_copy(
+            src_ref=tips.at[k],
+            dst_ref=(own_tips, nxt_tips)[section].at[k],
+            send_sem=tip_send.at[section, k],
+            recv_sem=(own_tip_recv, nxt_tip_recv)[section].at[k],
+            device_id=(sec - section, ty + dy, tx + dx),
+            device_id_type=MESH,
+        )
+
+    def diagonals(sign, do):
+        for k, (dy, dx) in enumerate(CORNERS):
+            @pl.when(there(sign * dy, sign * dx))
+            def _(k=k):
+                do(k)
+
     def up_down(ok, do):
         for dy in (-1, 1):
             @pl.when(ok(dy))
@@ -302,47 +395,34 @@
     def handed_on(dy):
         return jnp.logical_not(crosses(dy)) & there(dy, 0)
 
-    span = (rows + 2 * HALF) // 4
-    packed_lane = lax.broadcasted_iota(jnp.int32, (span, PATCH), 1)
-
-    def pack_columns(source, into):
-        for side, at in enumerate((PATCH, cols)):
-            first = 0 if side == 0 else PATCH - HALF
-            value = None
-            for q in range(4):
-                part = source[span * q : span * (q + 1), at : at + PATCH]
-                part = pltpu.roll(part, (HALF * q - first) % PATCH, 1) if HALF * q != first else part
-                value = part if q == 0 else jnp.where(packed_lane >= HALF * q, part, value)
-            into[side] = value
-
-    def unpack_columns(land, target):
-        for side, at in enumerate((PATCH + cols, 0)):
-            first = 0 if side == 0 else PATCH - HALF
-
-            @pl.when(there(0, 1 - 2 * side))
-            def _(side=side, at=at, first=first):
-                for q in range(4):
-                    part = land[side]
-                    part = pltpu.roll(part, (first - HALF * q) % PATCH, 1) if HALF * q != first else part
-                    target[span * q : span * (q + 1), at : at + PATCH] = part
-
     up_down(lambda dy: there(dy, 0), lambda dy: own_rows(dy).start())
+    sides(1, lambda dx: own_columns(dx).start())
+    diagonals(1, lambda k: tip_copy(k, 0).start())
 
     @pl.when(has_before)
     def _():
-        piece_copy(0).start()
-        piece_copy(1).start()
+        diagonals(1, lambda k: tip_copy(k, 1).start())
         up_down(straight, lambda dy: nxt_straight(dy).start())
 
-    tile.wait()
-    up_down(lambda dy: there(-dy, 0), lambda dy: own_rows(dy).wait_recv())
-    pack_columns(own, own_pack)
-    sides(1, lambda dx: own_columns(dx).start())
-
-    @pl.when(has_before)
-    def _():
-        for p in range(2, len(pieces)):
-            piece_copy(p).start()
+        @pl.when(crosses(-1))
+        def _():
+            piece_copy(1).start()
+
+        @pl.when(jnp.logical_not(crosses(-1)))
+        def _():
+            piece_copy(0).start()
+
+        piece_copy(2).start()
+
+        @pl.when(crosses(-1))
+        def _():
+            piece_copy(0).start()
+
+        @pl.when(jnp.logical_not(crosses(-1)))
+        def _():
+            piece_copy(1).start()
+
+        piece_copy(3).start()
 
     load.wait()
 
@@ -379,24 +459,33 @@
         return got[:PATCH] + got[PATCH:]
 
 
+    def hand_on(dy):
+        piece_copy((dy + 1) // 2).wait_recv()
+        nxt_rows(dy).start()
+
+    up_down(lambda dy: there(-dy, 0), lambda dy: own_rows(dy).wait_recv())
+    sides(-1, lambda dx: own_columns(dx).wait_recv())
+    diagonals(-1, lambda k: tip_copy(k, 0).wait_recv())
+    unpack_columns(own_land, own)
+    diagonals(-1, lambda k: unpack_tip(own_tips, own, k))
+
     @pl.when(has_next)
     def _():
-        piece_copy(0).wait_recv()
-        piece_copy(1).wait_recv()
-        up_down(handed_on, lambda dy: nxt_rows(dy).start())
-
-    sides(-1, lambda dx: own_columns(dx).wait_recv())
-    unpack_columns(own_land, own)
+        up_down(handed_on, hand_on)
 
     @pl.loop(0, node_rows + 1)
     def _(b):
         right_chunk(own, own_hi, own_lo, b, every)
-
 
     @pl.when(has_next)
     def _():
         piece_copy(2).wait_recv()
         sides(1, lambda dx: nxt_columns(dx).start())
+
+    @pl.when(has_before)
+    def _():
+        for p in range(4, len(pieces)):
+            piece_copy(p).start()
 
     @pl.loop(0, node_rows)
     def _(i):
@@ -404,10 +493,16 @@
             at = pl.ds(c, 2 * PATCH)
             spec[i, :, at] = left_spectrum(own_hi, own_lo, i, at)
 
-
     @pl.when(has_next)
     def _():
+        for dy in (-1, 1):
+            @pl.when(jnp.logical_not(handed_on(dy)))
+            def _(dy=dy):
+                piece_copy((dy + 1) // 2).wait_recv()
+
         up_down(lambda dy: there(-dy, 0), lambda dy: nxt_rows(dy).wait_recv())
+        diagonals(-1, lambda k: tip_copy(k, 1).wait_recv())
+        diagonals(-1, lambda k: unpack_tip(nxt_tips, nxt, k))
         sides(-1, lambda dx: nxt_columns(dx).wait_recv())
         unpack_columns(nxt_land, nxt)
 
@@ -450,24 +545,27 @@
     def _(step):
         @pl.when(step == 0)
         def _():
-            arrived(3)
+            arrived(3, 4)
+            unpack_rest(0)
             right_chunk(nxt, nxt_hi, nxt_lo, 1, every)
 
         @pl.when(step == 1)
         def _():
-            arrived(4)
+            arrived(5, 6)
+            unpack_rest(bands - 1)
             right_chunk(nxt, nxt_hi, nxt_lo, last, every)
 
         @pl.when(step == 2)
         def _():
             flows[1] = flow_block((0, last))
             flow_each(1, (True,), lambda k: flow_copy(k).start())
-            arrived(5, 6)
+            arrived(7, 8)
+            unpack_rest(middle)
             right_chunk(nxt, nxt_hi, nxt_lo, 2, parts[0])
 
         @pl.when(step == 3)
         def _():
-            arrived(7)
+            arrived(9)
             right_chunk(nxt, nxt_hi, nxt_lo, 2, parts[1])
 
         halves = [
@@ -503,12 +601,14 @@
 
     up_down(lambda dy: there(dy, 0), lambda dy: own_rows(dy).wait_send())
     sides(1, lambda dx: own_columns(dx).wait_send())
+    diagonals(1, lambda k: tip_copy(k, 0).wait_send())
 
     @pl.when(has_before)
     def _():
         for p in range(len(pieces)):
             piece_copy(p).wait_send()
         up_down(straight, lambda dy: nxt_straight(dy).wait_send())
+        diagonals(1, lambda k: tip_copy(k, 1).wait_send())
 
     @pl.when(has_next)
     def _():
@@ -596,7 +696,8 @@
         high = 2 * HALF + rows
         wide = node_cols * PATCH
         around = len(DIRECTIONS)
-        n_pieces = 8
+        n_pieces = 10
+        bands = (rows - 2 * HALF) // STRIDE
         dma = pltpu.SemaphoreType.DMA
         out = pl.pallas_call(
             functools.partial(kernel, sizes),
@@ -616,10 +717,15 @@
                 pltpu.VMEM((3, 8, PATCH), F32),
                 pltpu.VMEM((around, 8, PATCH), F32),
                 pltpu.VMEM((sizes[0], 8, PATCH), F32),
-                pltpu.VMEM((2, high // 4, PATCH), F32),
-                pltpu.VMEM((2, high // 4, PATCH), F32),
-                pltpu.VMEM((2, high // 4, PATCH), F32),
-                pltpu.VMEM((2, high // 4, PATCH), F32),
+                pltpu.VMEM((2, rows // 4, PATCH), F32),
+                pltpu.VMEM((2, rows // 4, PATCH), F32),
+                pltpu.VMEM((2, rows // 4, PATCH), F32),
+                pltpu.VMEM((2, rows // 4, PATCH), F32),
+                pltpu.VMEM((bands, STRIDE + HALF, PATCH), F32),
+                pltpu.VMEM((bands, STRIDE + HALF, PATCH), F32),
+                pltpu.VMEM((len(CORNERS), 8, PATCH), F32),
+                pltpu.VMEM((len(CORNERS), 8, PATCH), F32),
+                pltpu.VMEM((len(CORNERS), 8, PATCH), F32),
                 dma((2,)),
                 dma((n_pieces,)),
                 dma((n_pieces,)),
@@ -628,6 +734,9 @@
                 dma((4,)),
                 dma((4,)),
                 dma((2,)),
+                dma((2, len(CORNERS))),
+                dma((len(CORNERS),)),
+                dma((len(CORNERS),)),
                 dma((around,)),
                 dma((around,)),
                 dma((sizes[0],)),

time: 34.8 us -> 33.8 us (0.971)
  the two profiles are of different devices: /device:TPU:28 before, /device:TPU:92 now
where the time goes in v5:
time: 33.8 us; the launch traced here: 33.7 us
  Pallas kernels  31.8 us (94%)
  local copies, waits for them, and re-layouts  1.28 us (4%)
  between operations  0.64 us (2%)
    pallas_call x1, Pallas kernels, on_device(): pl.pallas_call(functools.partial(kernel, sizes), out_shape=jax.ShapeDtype...  31.8 us
    slice x1, local copies, waits for them, and re-layouts, on_device(): return (out[0], out[1])  1.28 us

profile of v5, /device:TPU:92, one launch (start us, length us, event | category | flops | bytes accessed | tf_op | source)
XLA Modules:
  0.0 33.7 jit_solution(17864910073784732372)
XLA Ops:
  0.6 31.8 %shard_map.41 = f32[2,8,128]{2,1,0:T(8,128)} custom-call(f32[256,512]{1,0:T(8,128)} %bitcast.3, bf16[4,256,256]{2,1,0:T(8,128)(2,1)} %constant.2.clone.tables_ref), custom_call_target="tpu_custom_call" | custom-call | tf_op jit(solution)/shard_map/pallas_call | solution.py:702
  32.4 1.3 %fusion = (f32[1,8,8]{2,1,0:T(8,128)}, f32[1,8,8]{2,1,0:T(8,128)}) fusion(f32[2,8,128]{2,1,0:T(8,128)} %shard_map.41), kind=kLoop, calls=%fused_computation | loop fusion | bytes 1024 | tf_op jit(solution)/shard_map/slice | solution.py:750

commit v6 on v5

--- a/solution.py
+++ b/solution.py
@@ -124,7 +124,7 @@
 def kernel(
     sizes, x_ref, tables_ref, out_ref, own, nxt, own_hi, own_lo, nxt_hi, nxt_lo, spec, table,
     stats, flows, around, meshes,
-    own_pack, own_land, nxt_pack, nxt_land, own_rest, nxt_rest, tips, own_tips, nxt_tips,
+    own_pack, own_land, nxt_pack, nxt_land, own_rest, nxt_rest, edges, tips, own_tips, nxt_tips,
     local_sem, piece_send, piece_recv, own_send, own_recv, nxt_send, nxt_recv, straight_send,
     tip_send, own_tip_recv, nxt_tip_recv,
     flow_send, flow_recv, mesh_send, mesh_recv,
@@ -149,6 +149,12 @@
 
     def crosses(dy):
         return (ty % 2 == 1) if dy > 0 else (ty % 2 == 0)
+
+    bands = (rows - 2 * HALF) // STRIDE
+    odd_core = ty % 2 == 1
+
+    def mirrored(k, count=bands):
+        return jnp.where(odd_core, count - 1 - k, k)
 
     def straight(dy):
         return crosses(dy) & there(dy, 0)
@@ -249,6 +255,12 @@
         own_rest[m, STRIDE : STRIDE + HALF] = jnp.where(
             lane[:HALF] < STRIDE, turned(left[:HALF], -HALF), turned(left[HALF:], HALF)
         )
+        left = own[r : r + STRIDE, 2 * PATCH : 3 * PATCH]
+        right = own[r : r + STRIDE, 3 * PATCH : 4 * PATCH]
+        lane = lane[:HALF]
+        low = jnp.where(lane < HALF, left[:HALF], turned(left[HALF:], HALF))
+        high = jnp.where(lane < PATCH - HALF, turned(right[:HALF], -HALF), right[HALF:])
+        own_rest[m, STRIDE + HALF : STRIDE + 2 * HALF] = jnp.where(lane < STRIDE, low, high)
 
     def unpack_rest(m):
         lane = lax.broadcasted_iota(jnp.int32, (HALF, PATCH), 1)
@@ -264,12 +276,24 @@
             nxt[HALF + r : 2 * HALF + r, PATCH : 2 * PATCH] = left
             nxt[HALF + r : 2 * HALF + r, cols : cols + PATCH] = right
 
+    def unpack_edges(m):
+        strip = nxt_rest[m, STRIDE + HALF : STRIDE + 2 * HALF]
+        edges[0] = jnp.concatenate([strip, turned(strip, -HALF)], axis=0)
+        edges[1] = jnp.concatenate([turned(strip, HALF), strip], axis=0)
+
+    def at_band(k, do):
+        for m in range(bands):
+            @pl.when(mirrored(k) == m)
+            def _(m=m):
+                do(m)
+
     tile.wait()
+    stats[...] = jnp.ones_like(stats)
     for side in range(2):
         own_pack[side] = packed(own, spans, side)
     for k, (dy, dx) in enumerate(CORNERS):
         tips[k] = packed(own, eighths(HALF if dy < 0 else rows), (dx + 1) // 2)
-    for m in range((rows - 2 * HALF) // STRIDE):
+    for m in range(bands):
         pack_rest(m)
 
     tall = 1 + (ty > 0).astype(jnp.int32) + (ty < n_ty - 1).astype(jnp.int32)
@@ -278,31 +302,30 @@
     ends = has_before.astype(jnp.int32) + has_next.astype(jnp.int32)
     pl.semaphore_wait(barrier, n_sec - 1 + tall * broad - 1 + (apart + (tall - 1) * (broad - 1)) * ends)
 
-    bands = (rows - 2 * HALF) // STRIDE
-    middle = bands // 2
-    pieces = [
-        (0, HALF, 0, cols),
-        (rows - HALF, HALF, 0, cols),
-        None,
-        0,
-        (HALF, STRIDE, PATCH, 2 * PATCH),
-        bands - 1,
-        (rows - HALF - STRIDE, STRIDE, PATCH, 2 * PATCH),
-        middle,
-        (HALF + middle * STRIDE, STRIDE, PATCH, PATCH),
-        (HALF + middle * STRIDE, STRIDE, 2 * PATCH, PATCH),
-    ]
+    banded = [mirrored(m) for m in range(bands)]
+
+    def band_rest(m, last):
+        return (banded[m], STRIDE + 2 * HALF if last else STRIDE + HALF)
+
+    def band_inner(m):
+        return (pl.multiple_of(HALF + banded[m] * STRIDE, HALF), STRIDE, PATCH, 2 * PATCH)
+
+    pieces = [(0, HALF, 0, cols), (rows - HALF, HALF, 0, cols), None]
+    for m in range(bands):
+        pieces += [band_rest(m, m == bands - 1), band_inner(m)]
 
     def piece_copy(p):
         piece = pieces[p]
         if piece is None:
             src, dst = own_pack, nxt_pack
-        elif isinstance(piece, int):
-            src, dst = own_rest.at[piece], nxt_rest.at[piece]
+        elif len(piece) == 2:
+            m, nr = piece
+            src, dst = own_rest.at[m, pl.ds(0, nr)], nxt_rest.at[m, pl.ds(0, nr)]
         else:
             r, nr, c, nc = piece
             src = x_ref.at[pl.ds(r, nr), pl.ds(c, nc)]
-            dst = nxt.at[pl.ds(HALF + r, nr), pl.ds(PATCH + c, nc)]
+            to = HALF + r if isinstance(r, int) else pl.multiple_of(HALF + r, HALF)
+            dst = nxt.at[pl.ds(to, nr), pl.ds(PATCH + c, nc)]
         return pltpu.make_async_remote_copy(
             src_ref=src,
             dst_ref=dst,
@@ -429,21 +452,23 @@
     lane = lax.broadcasted_iota(jnp.int32, (STRIDE, PATCH), 1)
     even, odd = lane < PATCH - HALF, lane >= HALF
 
-    order = [node_cols - 1, *range(node_cols - 1)]
+    order = [node_cols - 2, node_cols - 1, *range(node_cols - 2)]
     part_cols = node_cols // 2
     parts = (range(0, part_cols), range(part_cols, node_cols))
     every = range(node_cols)
 
-    def right_chunk(source, high, low, b, places):
+    def right_chunk(source, high, low, b, places, ahead=False):
         at = pl.ds(b * STRIDE if isinstance(b, int) else pl.multiple_of(b * STRIDE, STRIDE), STRIDE)
         patches = []
         for j in (order[p] for p in places):
             t = j // 2
             main = source[at, (t + 1) * PATCH : (t + 2) * PATCH]
-            if j % 2 == 0:
-                patch = jnp.where(even, main, source[at, t * PATCH : (t + 1) * PATCH])
+            beside = t if j % 2 == 0 else t + 2
+            if ahead and j in (1, node_cols - 2):
+                part = edges[0 if j == 1 else 1]
             else:
-                patch = jnp.where(odd, main, source[at, (t + 2) * PATCH : (t + 3) * PATCH])
+                part = source[at, beside * PATCH : (beside + 1) * PATCH]
+            patch = jnp.where(even if j % 2 == 0 else odd, main, part)
             patches.append(jnp.concatenate(split(patch), axis=1))
         got = jnp.dot(jnp.concatenate(patches, axis=0), table[0], preferred_element_type=F32)
         got = got[:, :PATCH] + got[:, PATCH:]
@@ -518,13 +543,18 @@
             inv = 1.0 / total
             columns = jnp.where(lanes == i, down * inv, columns)
             columns = jnp.where(lanes == node_rows + i, across * inv, columns)
-        columns = pltpu.roll(jnp.where(has_next, columns, 0.0), node_cols - 1, 0)
+        columns = pltpu.roll(jnp.where(has_next, columns, 0.0), node_cols - 2, 0)
         return jnp.transpose(jnp.concatenate([columns] * 16, axis=0))[:8]
+
+    def flow_stage(dy, dx):
+        if dy == 0:
+            return 2
+        return jnp.where(crosses(dy), 1, 0 if dx == 0 else 2)
 
     def flow_copy(index):
         dy, dx = DIRECTIONS[index]
         return pltpu.make_async_remote_copy(
-            src_ref=flows.at[1 if dy and dx else 0],
+            src_ref=flows.at[flow_stage(dy, dx)],
             dst_ref=around.at[index],
             send_sem=flow_send.at[index],
             recv_sem=flow_recv.at[index],
@@ -532,44 +562,53 @@
             device_id_type=MESH,
         )
 
-    def flow_each(sign, corners, do):
+    def flow_each(sign, do, stage=None):
         for index, (dy, dx) in enumerate(DIRECTIONS):
-            if bool(dy and dx) in corners:
-                @pl.when(there(sign * dy, sign * dx))
-                def _(index=index):
-                    do(index)
-
-    last = node_rows - 1
+            ok = there(sign * dy, sign * dx)
+            if stage is not None:
+                ok = ok & (flow_stage(dy, dx) == stage)
+
+            @pl.when(ok)
+            def _(index=index):
+                do(index)
+
+    def flow_send_stage(stage):
+        flows[stage] = flow_block(range(node_rows))
+        flow_each(1, lambda k: flow_copy(k).start(), stage)
 
     @pl.loop(0, 4)
     def _(step):
         @pl.when(step == 0)
         def _():
             arrived(3, 4)
-            unpack_rest(0)
-            right_chunk(nxt, nxt_hi, nxt_lo, 1, every)
+            at_band(0, unpack_rest)
 
         @pl.when(step == 1)
         def _():
             arrived(5, 6)
-            unpack_rest(bands - 1)
-            right_chunk(nxt, nxt_hi, nxt_lo, last, every)
+            at_band(1, unpack_rest)
+
+        @pl.when(step < 2)
+        def _():
+            right_chunk(nxt, nxt_hi, nxt_lo, 1 + mirrored(step), every)
 
         @pl.when(step == 2)
         def _():
-            flows[1] = flow_block((0, last))
-            flow_each(1, (True,), lambda k: flow_copy(k).start())
-            arrived(7, 8)
-            unpack_rest(middle)
-            right_chunk(nxt, nxt_hi, nxt_lo, 2, parts[0])
+            flow_send_stage(1)
+            arrived(7)
+            at_band(2, unpack_rest)
+            at_band(2, unpack_edges)
+            right_chunk(nxt, nxt_hi, nxt_lo, 1 + mirrored(2), parts[0], True)
 
         @pl.when(step == 3)
         def _():
-            arrived(9)
-            right_chunk(nxt, nxt_hi, nxt_lo, 2, parts[1])
+            flow_send_stage(2)
+            arrived(8)
+            right_chunk(nxt, nxt_hi, nxt_lo, 1 + mirrored(2), parts[1])
 
         halves = [
-            (jnp.where(step < 2, step * last, 1 + h), jnp.where(step < 2, h, step - 2)) for h in range(2)
+            (mirrored(jnp.where(step < 2, step, 2 + h), node_rows), jnp.where(step < 2, h, step - 2))
+            for h in range(2)
         ]
         nodes = [slice(n * PATCH, (n + 1) * PATCH) for n in range(node_cols)]
         mine, other = [], []
@@ -597,7 +636,7 @@
 
     block = flow_block(range(node_rows))
     flows[0] = block
-    flow_each(1, (False,), lambda k: flow_copy(k).start())
+    flow_each(1, lambda k: flow_copy(k).start(), 0)
 
     up_down(lambda dy: there(dy, 0), lambda dy: own_rows(dy).wait_send())
     sides(1, lambda dx: own_columns(dx).wait_send())
@@ -615,7 +654,7 @@
         up_down(handed_on, lambda dy: nxt_rows(dy).wait_send())
         sides(1, lambda dx: nxt_columns(dx).wait_send())
 
-    flow_each(-1, (True, False), lambda k: flow_copy(k).wait_recv())
+    flow_each(-1, lambda k: flow_copy(k).wait_recv())
 
     lines = {}
     for dy in (-1, 0, 1):
@@ -642,11 +681,11 @@
     result = jnp.where(
         subs < node_rows, pltpu.roll(done[0], 6, 0), pltpu.roll(done[1], (8 + node_rows - 2) % 8, 0)
     )
-    flows[2] = result
+    flows[3] = result
 
     def mesh_copy(d):
         return pltpu.make_async_remote_copy(
-            src_ref=flows.at[2],
+            src_ref=flows.at[3],
             dst_ref=meshes.at[sec],
             send_sem=mesh_send.at[d],
             recv_sem=mesh_recv.at[d],
@@ -656,7 +695,7 @@
 
     def mesh_wait(d):
         pltpu.make_async_remote_copy(
-            src_ref=flows.at[2],
+            src_ref=flows.at[3],
             dst_ref=meshes.at[sec - d],
             send_sem=mesh_send.at[d],
             recv_sem=mesh_recv.at[d],
@@ -679,7 +718,7 @@
     out_ref[0] = result
     out_ref[1] = earlier
 
-    flow_each(1, (True, False), lambda k: flow_copy(k).wait_send())
+    flow_each(1, lambda k: flow_copy(k).wait_send())
     for d in range(1, n_sec):
         @pl.when(sec + d < n_sec)
         def _(d=d):
@@ -696,8 +735,8 @@
         high = 2 * HALF + rows
         wide = node_cols * PATCH
         around = len(DIRECTIONS)
-        n_pieces = 10
         bands = (rows - 2 * HALF) // STRIDE
+        n_pieces = 3 + 2 * bands
         dma = pltpu.SemaphoreType.DMA
         out = pl.pallas_call(
             functools.partial(kernel, sizes),
@@ -714,15 +753,16 @@
                 pltpu.VMEM((node_rows, PATCH, wide), F32),
                 pltpu.VMEM((4, 2 * PATCH, 2 * PATCH), BF16),
                 pltpu.VMEM((3, node_rows, node_cols, PATCH), F32),
-                pltpu.VMEM((3, 8, PATCH), F32),
+                pltpu.VMEM((4, 8, PATCH), F32),
                 pltpu.VMEM((around, 8, PATCH), F32),
                 pltpu.VMEM((sizes[0], 8, PATCH), F32),
                 pltpu.VMEM((2, rows // 4, PATCH), F32),
                 pltpu.VMEM((2, rows // 4, PATCH), F32),
                 pltpu.VMEM((2, rows // 4, PATCH), F32),
                 pltpu.VMEM((2, rows // 4, PATCH), F32),
-                pltpu.VMEM((bands, STRIDE + HALF, PATCH), F32),
-                pltpu.VMEM((bands, STRIDE + HALF, PATCH), F32),
+                pltpu.VMEM((bands, STRIDE + 2 * HALF, PATCH), F32),
+                pltpu.VMEM((bands, STRIDE + 2 * HALF, PATCH), F32),
+                pltpu.VMEM((2, STRIDE, PATCH), F32),
                 pltpu.VMEM((len(CORNERS), 8, PATCH), F32),
                 pltpu.VMEM((len(CORNERS), 8, PATCH), F32),
                 pltpu.VMEM((len(CORNERS), 8, PATCH), F32),

time: 33.8 us -> 32.7 us (0.967)
  Pallas kernels: 31.8 us -> 30.6 us
    pallas_call x1, Pallas kernels: 31.8 us -> 30.6 us  [on_device(): pl.pallas_call(functools.partial(kernel, sizes), out_shape=jax.ShapeDtype...]
where the time goes in v6:
time: 32.7 us; the launch traced here: 32.5 us
  Pallas kernels  30.6 us (94%)
  local copies, waits for them, and re-layouts  1.28 us (4%)
  between operations  0.64 us (2%)
    pallas_call x1, Pallas kernels, on_device(): pl.pallas_call(functools.partial(kernel, sizes), out_shape=jax.ShapeDtype...  30.6 us
    slice x1, local copies, waits for them, and re-layouts, on_device(): return (out[0], out[1])  1.28 us

profile of v6, /device:TPU:92, one launch (start us, length us, event | category | flops | bytes accessed | tf_op | source)
XLA Modules:
  0.0 32.5 jit_solution(5491883546518323526)
XLA Ops:
  0.6 30.6 %shard_map.41 = f32[2,8,128]{2,1,0:T(8,128)} custom-call(f32[256,512]{1,0:T(8,128)} %bitcast.3, bf16[4,256,256]{2,1,0:T(8,128)(2,1)} %constant.2.clone.tables_ref), custom_call_target="tpu_custom_call" | custom-call | tf_op jit(solution)/shard_map/pallas_call | solution.py:741
  31.2 1.3 %fusion = (f32[1,8,8]{2,1,0:T(8,128)}, f32[1,8,8]{2,1,0:T(8,128)}) fusion(f32[2,8,128]{2,1,0:T(8,128)} %shard_map.41), kind=kLoop, calls=%fused_computation | loop fusion | bytes 1024 | tf_op jit(solution)/shard_map/slice | solution.py:790

commit v7 on v6

--- a/solution.py
+++ b/solution.py
@@ -169,15 +169,12 @@
     for dy, dx in DIRECTIONS:
         greet(there(dy, dx), sec, ty + dy, tx + dx)
     for dy in (-1, 1):
-        greet(has_before & straight(dy), sec - 1, ty + dy, tx)
         greet(has_next & straight(dy), sec + 1, ty + dy, tx)
     for dy, dx in CORNERS:
-        greet(has_before & there(dy, dx), sec - 1, ty + dy, tx + dx)
         greet(has_next & there(dy, dx), sec + 1, ty + dy, tx + dx)
+    greet(has_next, sec + 1, ty, tx)
     for d in range(1, n_sec):
-        pl.semaphore_signal(
-            barrier, inc=1, device_id=(lax.rem(sec + d, n_sec), ty, tx), device_id_type=MESH
-        )
+        greet(sec - d >= 0, sec - d, ty, tx)
 
     tile = pltpu.make_async_copy(
         x_ref, own.at[pl.ds(HALF, rows), pl.ds(PATCH, cols)], local_sem.at[0]
@@ -299,8 +296,8 @@
     tall = 1 + (ty > 0).astype(jnp.int32) + (ty < n_ty - 1).astype(jnp.int32)
     broad = 1 + (tx > 0).astype(jnp.int32) + (tx < n_tx - 1).astype(jnp.int32)
     apart = (crosses(-1) & there(-1, 0)).astype(jnp.int32) + (crosses(1) & there(1, 0)).astype(jnp.int32)
-    ends = has_before.astype(jnp.int32) + has_next.astype(jnp.int32)
-    pl.semaphore_wait(barrier, n_sec - 1 + tall * broad - 1 + (apart + (tall - 1) * (broad - 1)) * ends)
+    back = has_before.astype(jnp.int32) * (1 + apart + (tall - 1) * (broad - 1))
+    pl.semaphore_wait(barrier, tall * broad - 1 + back + n_sec - 1 - sec)
 
     banded = [mirrored(m) for m in range(bands)]
 
@@ -445,7 +442,8 @@
         def _():
             piece_copy(1).start()
 
-        piece_copy(3).start()
+        for p in range(3, len(pieces)):
+            piece_copy(p).start()
 
     load.wait()
 
@@ -506,11 +504,6 @@
     def _():
         piece_copy(2).wait_recv()
         sides(1, lambda dx: nxt_columns(dx).start())
-
-    @pl.when(has_before)
-    def _():
-        for p in range(4, len(pieces)):
-            piece_copy(p).start()
 
     @pl.loop(0, node_rows)
     def _(i):

time: 32.7 us -> 32.3 us (0.988)
    pallas_call x1, Pallas kernels: 30.6 us -> 30.3 us  [on_device(): pl.pallas_call(functools.partial(kernel, sizes), out_shape=jax.ShapeDtype...]
where the time goes in v7:
time: 32.3 us; the launch traced here: 32.2 us
  Pallas kernels  30.3 us (94%)
  local copies, waits for them, and re-layouts  1.28 us (4%)
  between operations  0.64 us (2%)
    pallas_call x1, Pallas kernels, on_device(): pl.pallas_call(functools.partial(kernel, sizes), out_shape=jax.ShapeDtype...  30.3 us
    slice x1, local copies, waits for them, and re-layouts, on_device(): return (out[0], out[1])  1.28 us

profile of v7, /device:TPU:92, one launch (start us, length us, event | category | flops | bytes accessed | tf_op | source)
XLA Modules:
  0.0 32.2 jit_solution(4154295775574024077)
XLA Ops:
  0.6 30.3 %shard_map.41 = f32[2,8,128]{2,1,0:T(8,128)} custom-call(f32[256,512]{1,0:T(8,128)} %bitcast.3, bf16[4,256,256]{2,1,0:T(8,128)(2,1)} %constant.2.clone.tables_ref), custom_call_target="tpu_custom_call" | custom-call | tf_op jit(solution)/shard_map/pallas_call | solution.py:734
  30.9 1.3 %fusion = (f32[1,8,8]{2,1,0:T(8,128)}, f32[1,8,8]{2,1,0:T(8,128)}) fusion(f32[2,8,128]{2,1,0:T(8,128)} %shard_map.41), kind=kLoop, calls=%fused_computation | loop fusion | bytes 1024 | tf_op jit(solution)/shard_map/slice | solution.py:783

commit v8 on v7

--- a/solution.py
+++ b/solution.py
@@ -60,7 +60,7 @@
     return high, low
 
 
-def product(own, other):
+def product(own, turned, other):
     half = PATCH // 2
     lane = lax.broadcasted_iota(jnp.int32, (half, PATCH), 1)
     row = lax.broadcasted_iota(jnp.int32, (half, PATCH), 0)
@@ -70,18 +70,17 @@
     top_row = row == 0
     t, u = own[:half], own[half:]
     t2, u2 = other[:half], other[half:]
-    rt2 = pltpu.roll(t2, half, 1)
-    ru2 = pltpu.roll(u2, half, 1)
-    uu, uru = u * u2, u * ru2
+    rt, ru = turned[:half], turned[half:]
+    uu, uru = u * u2, ru * u2
     g = t * t2 + jnp.where(top_row, 0.0, uu)
-    h = t * rt2 + jnp.where(top_row, 0.0, uru)
+    h = rt * t2 + jnp.where(top_row, 0.0, uru)
     g2 = jnp.where(top_row, uu, t * u2 - u * t2)
-    h2 = jnp.where(top_row, uru, t * ru2 - u * rt2)
+    h2 = jnp.where(top_row, uru, rt * u2 - ru * t2)
 
     def joined(g, h):
         cross = pltpu.roll(jnp.where(left, h, g), half, 1)
         cross = jnp.where(alone, 0.0, cross)
-        return jnp.where(plain, cross + g, cross - h)
+        return jnp.where(plain, g + cross, h - cross)
 
     top = joined(g, h)
     top = jnp.where(top_row & (lane == 0), 0.0, top)
@@ -509,7 +508,12 @@
     def _(i):
         for c in range(0, wide, 2 * PATCH):
             at = pl.ds(c, 2 * PATCH)
-            spec[i, :, at] = left_spectrum(own_hi, own_lo, i, at)
+            got = left_spectrum(own_hi, own_lo, i, at)
+            spec[i, 0, :, at] = got
+            for n in range(2):
+                spec[i, 1, :, pl.ds(c + n * PATCH, PATCH)] = pltpu.roll(
+                    got[:, n * PATCH : (n + 1) * PATCH], PATCH // 2, 1
+                )
 
     @pl.when(has_next)
     def _():
@@ -604,13 +608,14 @@
             for h in range(2)
         ]
         nodes = [slice(n * PATCH, (n + 1) * PATCH) for n in range(node_cols)]
-        mine, other = [], []
+        mine, swapped, other = [], [], []
         for i, g in halves:
             columns = pl.ds(pl.multiple_of(g * part_cols * PATCH, PATCH), part_cols * PATCH)
             other.append(left_spectrum(nxt_hi, nxt_lo, i, columns))
-            mine.append(spec[i, :, columns])
-        mine, other = (jnp.concatenate(value, axis=1) for value in (mine, other))
-        prods = jnp.concatenate([product(mine[:, n], other[:, n]) for n in nodes], axis=1)
+            mine.append(spec[i, 0, :, columns])
+            swapped.append(spec[i, 1, :, columns])
+        mine, swapped, other = (jnp.concatenate(value, axis=1) for value in (mine, swapped, other))
+        prods = jnp.concatenate([product(mine[:, n], swapped[:, n], other[:, n]) for n in nodes], axis=1)
         mixed = jnp.dot(
             table[2], jnp.concatenate(split(prods), axis=0), preferred_element_type=F32
         )
@@ -743,7 +748,7 @@
                 pltpu.VMEM((high, wide), BF16),
                 pltpu.VMEM((high, wide), BF16),
                 pltpu.VMEM((high, wide), BF16),
-                pltpu.VMEM((node_rows, PATCH, wide), F32),
+                pltpu.VMEM((node_rows, 2, PATCH, wide), F32),
                 pltpu.VMEM((4, 2 * PATCH, 2 * PATCH), BF16),
                 pltpu.VMEM((3, node_rows, node_cols, PATCH), F32),
                 pltpu.VMEM((4, 8, PATCH), F32),

time: 32.3 us -> 32.1 us (level)
  no operation moved by 1% of the time
where the time goes in v8:
time: 32.1 us; the launch traced here: 31.9 us
  Pallas kernels  30 us (93%)
  local copies, waits for them, and re-layouts  1.28 us (4%)
  between operations  0.64 us (2%)
    pallas_call x1, Pallas kernels, on_device(): pl.pallas_call(functools.partial(kernel, sizes), out_shape=jax.ShapeDtype...  30 us
    slice x1, local copies, waits for them, and re-layouts, on_device(): return (out[0], out[1])  1.28 us

profile of v8, /device:TPU:92, one launch (start us, length us, event | category | flops | bytes accessed | tf_op | source)
XLA Modules:
  0.0 31.9 jit_solution(14662554007362194978)
XLA Ops:
  0.6 30.0 %shard_map.41 = f32[2,8,128]{2,1,0:T(8,128)} custom-call(f32[256,512]{1,0:T(8,128)} %bitcast.3, bf16[4,256,256]{2,1,0:T(8,128)(2,1)} %constant.2.clone.tables_ref), custom_call_target="tpu_custom_call" | custom-call | tf_op jit(solution)/shard_map/pallas_call | solution.py:739
  30.7 1.3 %fusion = (f32[1,8,8]{2,1,0:T(8,128)}, f32[1,8,8]{2,1,0:T(8,128)}) fusion(f32[2,8,128]{2,1,0:T(8,128)} %shard_map.41), kind=kLoop, calls=%fused_computation | loop fusion | bytes 1024 | tf_op jit(solution)/shard_map/slice | solution.py:788

commit v9 on v8

--- a/solution.py
+++ b/solution.py
@@ -67,15 +67,21 @@
     left = lane < half
     alone = (lane == 0) | (lane == half)
     plain = left | alone
-    top_row = row == 0
+    top_row = row[:8] == 0
+
+    def first_row(value, rest):
+        head = jnp.where(top_row, value[:8], rest[:8])
+        return jnp.concatenate([head, rest[8:]], axis=0)
+
+    none = jnp.zeros((8, PATCH), F32)
     t, u = own[:half], own[half:]
     t2, u2 = other[:half], other[half:]
     rt, ru = turned[:half], turned[half:]
     uu, uru = u * u2, ru * u2
-    g = t * t2 + jnp.where(top_row, 0.0, uu)
-    h = rt * t2 + jnp.where(top_row, 0.0, uru)
-    g2 = jnp.where(top_row, uu, t * u2 - u * t2)
-    h2 = jnp.where(top_row, uru, rt * u2 - ru * t2)
+    g = t * t2 + first_row(none, uu)
+    h = rt * t2 + first_row(none, uru)
+    g2 = first_row(uu, t * u2 - u * t2)
+    h2 = first_row(uru, rt * u2 - ru * t2)
 
     def joined(g, h):
         cross = pltpu.roll(jnp.where(left, h, g), half, 1)
@@ -83,7 +89,8 @@
         return jnp.where(plain, g + cross, h - cross)
 
     top = joined(g, h)
-    top = jnp.where(top_row & (lane == 0), 0.0, top)
+    head = jnp.where(top_row & (lane[:8] == 0), 0.0, top[:8])
+    top = jnp.concatenate([head, top[8:]], axis=0)
     return jnp.concatenate([top, joined(g2, h2)], axis=0)
 
 

time: 32.1 us -> 32.1 us (level)
  no operation moved by 1% of the time
where the time goes in v9:
time: 32.1 us; the launch traced here: 31.9 us
  Pallas kernels  30 us (93%)
  local copies, waits for them, and re-layouts  1.28 us (4%)
  between operations  0.64 us (2%)
    pallas_call x1, Pallas kernels, on_device(): pl.pallas_call(functools.partial(kernel, sizes), out_shape=jax.ShapeDtype...  30 us
    slice x1, local copies, waits for them, and re-layouts, on_device(): return (out[0], out[1])  1.28 us

profile of v9, /device:TPU:92, one launch (start us, length us, event | category | flops | bytes accessed | tf_op | source)
XLA Modules:
  0.0 31.9 jit_solution(14662554007362194978)
XLA Ops:
  0.6 30.0 %shard_map.41 = f32[2,8,128]{2,1,0:T(8,128)} custom-call(f32[256,512]{1,0:T(8,128)} %bitcast.3, bf16[4,256,256]{2,1,0:T(8,128)(2,1)} %constant.2.clone.tables_ref), custom_call_target="tpu_custom_call" | custom-call | tf_op jit(solution)/shard_map/pallas_call | solution.py:746
  30.7 1.3 %fusion = (f32[1,8,8]{2,1,0:T(8,128)}, f32[1,8,8]{2,1,0:T(8,128)}) fusion(f32[2,8,128]{2,1,0:T(8,128)} %shard_map.41), kind=kLoop, calls=%fused_computation | loop fusion | bytes 1024 | tf_op jit(solution)/shard_map/slice | solution.py:795
